TPU v7x, 128 devices: a whole 4x4x4 slice. The times are simulated.
128 devices in a mesh: grp: 8 (over x, core), blk: 16 (over y, z).
Axes of the slice: x: 4, y: 4, z: 4, core: 2. Of those that a mesh axis runs over, the one named last changes fastest.
Arguments:
- img_feats: bfloat16 [16384, 1024], P(('grp', 'blk')), may hold values from -8 to 8
- txt_feats: bfloat16 [16384, 1024], P(('grp', 'blk')), may hold values from -8 to 8
- img_head: bfloat16 [1024, 1024], replicated, may hold values from -1 to 1
- txt_head: bfloat16 [1024, 1024], replicated, may hold values from -1 to 1
- cluster_ids: int32 [16384, 1], P(('grp', 'blk')), may hold values from 0 to 127; in each aligned block of 128 rows (0 to 127, 128 to 255, ...) at most 2 rows name the same one
- placement: int32 [128], replicated, may hold values from 0 to 127, each once
- log_scale: float32 [1], replicated, may hold values from 2.3 to 2.9
- bias: float32 [1], replicated, may hold values from -6 to -3
Outputs:
- img_feat_grad: float32 [16384, 1024], P(('grp', 'blk'))
- txt_feat_grad: float32 [16384, 1024], P(('grp', 'blk'))
- pair_loss: float32 [16384], P(('grp', 'blk'))
Inputs may be any that keep to these rules, and one draw needn't show every extreme that they name: `cluster_ids`: among the rows of one device at most 2 pairs name the same cluster, a bound that some block reaches of them; over all 16384 pairs every cluster is named by some pair. Each device index along grp+blk (grp slowest) appears once; the pairs of cluster c are gathered on the device of index placement[c], of team placement[c] // 16.
All inputs are finite; a program needn't handle non-finite values.
Results may differ from a plain program's by a relative error of at most 0.0025.
Values may be sent and summed in bfloat16 or wider, within the bound.
A program may use at most 128 MiB of HBM per device.

v0:
```python
import jax
import jax.numpy as jnp
from jax import lax
from jax.sharding import PartitionSpec as P

EPS = 1e-06


def unit_rows(feats, head):
    raw = jnp.dot(feats, head, preferred_element_type=jnp.float32)
    factor = lax.rsqrt(jnp.sum(raw * raw, axis=1, keepdims=True) + EPS)
    return (raw * factor, factor)


def tile_terms(images, image_live, texts, text_live, row_start, scale_t, shift):
    sims = lax.dot_general(
        images, texts, (((1,), (1,)), ((), ())), preferred_element_type=jnp.float32
    )
    logits = scale_t * sims + shift
    row_ids = row_start + jnp.arange(images.shape[0], dtype=jnp.int32)
    col_ids = jnp.arange(texts.shape[0], dtype=jnp.int32)
    sign = jnp.where(row_ids[:, None] == col_ids[None, :], 1.0, -1.0).astype(jnp.float32)
    live = image_live.astype(jnp.float32)[:, None] * text_live.astype(jnp.float32)[None, :]
    losses = -jax.nn.log_sigmoid(sign * logits) * live
    weights = (scale_t * -sign * jax.nn.sigmoid(-sign * logits) * live).astype(jnp.bfloat16)
    return (weights, jnp.sum(losses, axis=1))


def unit_backward(grad, unit, factor, head):
    along = jnp.sum(unit * grad, axis=1, keepdims=True)
    local = ((grad - unit * along) * factor).astype(jnp.bfloat16)
    return lax.dot_general(
        local, head, (((1,), (1,)), ((), ())), preferred_element_type=jnp.float32
    )


def body(img_feats, txt_feats, img_head, txt_head, cluster_ids, placement, log_scale, bias):
    devices = lax.axis_size(("grp", "blk"))
    cycle_size = lax.axis_size("blk")
    pairs = img_feats.shape[0]
    width = img_head.shape[1]
    slot = max(2, 3 * pairs // (2 * devices))
    rows = devices * slot
    scale_t = jnp.exp(log_scale[0])
    shift = bias[0]
    img_unit, img_factor = unit_rows(img_feats, img_head)
    txt_unit, txt_factor = unit_rows(txt_feats, txt_head)
    cluster_range = jnp.arange(placement.shape[0], dtype=jnp.int32)
    target = jnp.sum(
        jnp.where(cluster_ids == cluster_range[None, :], placement[None, :], 0), axis=1
    )
    owner_hits = (target[:, None] == jnp.arange(devices, dtype=jnp.int32)[None, :]).astype(
        jnp.int32
    )
    earlier = jnp.cumsum(owner_hits, axis=0) - owner_hits
    position = target * slot + jnp.sum(earlier * owner_hits, axis=1)
    layout = (jnp.arange(rows, dtype=jnp.int32)[:, None] == position[None, :]).astype(jnp.bfloat16)
    send_img = jnp.dot(
        layout, img_unit.astype(jnp.bfloat16), preferred_element_type=jnp.float32
    ).astype(jnp.bfloat16)
    send_txt = jnp.dot(
        layout, txt_unit.astype(jnp.bfloat16), preferred_element_type=jnp.float32
    ).astype(jnp.bfloat16)
    send_live = jnp.sum(layout.astype(jnp.float32), axis=1).astype(jnp.bfloat16)
    got_img, got_txt, got_live = (
        lax.all_to_all(
            send_img.reshape(devices, slot, width),
            ("grp", "blk"),
            split_axis=0,
            concat_axis=0,
            tiled=True,
        ),
        lax.all_to_all(
            send_txt.reshape(devices, slot, width),
            ("grp", "blk"),
            split_axis=0,
            concat_axis=0,
            tiled=True,
        ),
        lax.all_to_all(
            send_live.reshape(devices, slot),
            ("grp", "blk"),
            split_axis=0,
            concat_axis=0,
            tiled=True,
        ),
    )
    recv_img = got_img.reshape(rows, width)
    recv_txt = got_txt.reshape(rows, width)
    recv_live = got_live.reshape(rows)
    own_start = lax.axis_index("blk") * rows
    texts_all, live_all = (
        lax.all_gather(recv_txt, "blk", axis=0, tiled=True),
        lax.all_gather(recv_live, "blk", axis=0, tiled=True),
    )
    weights, row_loss = tile_terms(
        recv_img, recv_live, texts_all, live_all, own_start, scale_t, shift
    )
    img_grad = jnp.dot(weights, texts_all, preferred_element_type=jnp.float32)
    txt_grad = lax.psum_scatter(
        lax.dot_general(
            weights, recv_img, (((0,), (0,)), ((), ())), preferred_element_type=jnp.float32
        ),
        "blk",
        scatter_dimension=0,
        tiled=True,
    )
    row_loss = row_loss / (cycle_size * pairs)
    back_img, back_txt, back_loss = (
        lax.all_to_all(
            img_grad.reshape(devices, slot, width),
            ("grp", "blk"),
            split_axis=0,
            concat_axis=0,
            tiled=True,
        ),
        lax.all_to_all(
            txt_grad.reshape(devices, slot, width),
            ("grp", "blk"),
            split_axis=0,
            concat_axis=0,
            tiled=True,
        ),
        lax.all_to_all(
            row_loss.reshape(devices, slot), ("grp", "blk"), split_axis=0, concat_axis=0, tiled=True
        ),
    )
    emb_grad_img = jnp.take(back_img.reshape(rows, width), position, axis=0)
    emb_grad_txt = jnp.take(back_txt.reshape(rows, width), position, axis=0)
    pair_loss = jnp.take(back_loss.reshape(rows), position, axis=0)
    img_feat_grad = unit_backward(emb_grad_img, img_unit, img_factor, img_head)
    txt_feat_grad = unit_backward(emb_grad_txt, txt_unit, txt_factor, txt_head)
    return (img_feat_grad, txt_feat_grad, pair_loss)


def solution(mesh):
    placed = (
        P(("grp", "blk"), None),
        P(("grp", "blk"), None),
        P(),
        P(),
        P(("grp", "blk"), None),
        P(),
        P(),
        P(),
    )
    return jax.shard_map(
        body,
        mesh=mesh,
        in_specs=placed,
        out_specs=(P(("grp", "blk"), None), P(("grp", "blk"), None), P(("grp", "blk"))),
        check_vma=False,
    )
```

profile of v0, /device:TPU:1, one launch (start us, length us, event | category | flops | bytes accessed | tf_op | source)
XLA Modules:
  0.0 297.9 jit_solution(4415942225144075186)
XLA Ops:
  7.2 0.0 copy-start
  7.2 0.0 all-gather.3.cloned.1.call-start
  7.2 1.0 select_reduce_fusion.1
  8.2 0.1 fusion.27
  8.3 0.2 reduce_window_sum.11
  8.5 0.2 select_reduce_fusion
  8.7 0.1 copy-done
  8.8 1.5 multiply_reduce_fusion.3
  10.3 2.4 multiply_reduce_fusion.2
  12.7 0.0 copy-start.2
  12.7 0.8 copy-done.2
  13.5 0.3 convolution_convert_fusion
  13.8 1.0 reshape.131
  14.8 25.4 %all_to_all.36 = bf16[128,2,1024]{2,1,0:T(2,128)(2,1)S(1)} all-to-all(bf16[128,2,1024]{2,1,0:T(2,128)(2,1)} %reshape.131), channel_id=1, replica_groups=mesh['grp'=8,'blk'=16] {'grp','blk'}, dimensions={0} | all-to-all | bytes 1048576 | tf_op jit(solution)/shard_map/all_to_all | solution.py:73
  40.2 1.0 reshape.132
  41.2 0.0 all-gather.3.cloned.1.call-update
  41.2 0.1 fusion.24
  41.3 0.8 all_to_all.29
  42.2 4.2 %all-to-all-start.2 = ((bf16[128,1,2]{2,1,0:T(2,128)(2,1)}), bf16[128,1,2]{2,1,0:T(2,128)(2,1)S(1)}, u32[]{:S(2)}, u32[]{:S(2)}) async-start(bf16[128,1,2]{2,1,0:T(2,128)(2,1)} %all_to_all.29), calls=%async_computation.2 | async-start | bytes 131072 | tf_op jit(solution)/shard_map/all_to_all | solution.py:80
  46.3 0.3 convolution_convert_fusion.1
  46.7 0.0 copy-done.4
  46.7 1.0 reshape.129
  47.7 8.3 %all-to-all-done.2 = bf16[128,1,2]{2,1,0:T(2,128)(2,1)S(1)} async-done(((bf16[128,1,2]{2,1,0:T(2,128)(2,1)}), bf16[128,1,2]{2,1,0:T(2,128)(2,1)S(1)}, u32[]{:S(2)}, u32[]{:S(2)}) %all-to-all-start.2) | async-done | bytes 544 | tf_op jit(solution)/shard_map/all_to_all | solution.py:80
  56.0 4.5 %all-to-all-start = ((bf16[128,2,1024]{2,1,0:T(2,128)(2,1)}), bf16[128,2,1024]{2,1,0:T(2,128)(2,1)S(1)}, u32[]{:S(2)}, u32[]{:S(2)}) async-start(bf16[128,2,1024]{2,1,0:T(2,128)(2,1)} %reshape.129), calls=%async_computation | async-start | bytes 1048576 | tf_op jit(solution)/shard_map/all_to_all | solution.py:66
  60.5 0.0 reduce-scatter.2.cloned.1.call-start
  61.9 0.2 reduce.2
  62.1 0.1 reshape.165
  62.2 0.2 convert_reduce_fusion
  62.4 0.1 reshape.169
  62.6 20.2 %all-gather = bf16[16,1,256]{2,1,0:T(2,128)(2,1)S(1)} all-gather(bf16[1,1,256]{2,1,0:T(2,128)(2,1)S(1)} %reshape.165), channel_id=1, replica_groups=mesh['grp'=8,'blk'=16] {'blk'}, dimensions={0}, use_global_device_ids=true | all-gather | bytes 8704 | tf_op jit(solution)/shard_map/all_gather | solution.py:94
  82.8 0.0 all-to-all-done
  82.8 0.2 reshape.130
  83.0 28.7 %all-gather.3.cloned.1.call-done = bf16[4096,1024]{1,0:T(8,128)(2,1)} async-done(((bf16[256,1024]{1,0:T(8,128)(2,1)}), bf16[4096,1024]{1,0:T(8,128)(2,1)}) %all-gather.3.cloned.1.call-update) | async-done | bytes 8388624 | tf_op jit(solution)/shard_map/all_gather | solution.py:93
  111.6 7.9 %fusion.9 = (f32[256]{0:T(256)S(1)}, f32[256,4096]{1,0:T(8,128)S(1)}) fusion(f32[4096]{0:T(1024)S(1)} %bitcast.20, f32[256]{0:T(256)S(1)} %reshape.169, s32[256]{0:T(256)S(1)} %iota_add_fusion, f32[]{:T(128)} %bitcast.19, bf16[256,1024]{1,0:T(8,128)(2,1)S(1)} %reshape.130, bf16[4096,1024]{1,0:T(8,128)(2,1)} %all-gather.3.cloned.1.call-done, f32[]{:T(128)} %bitcast.1), kind=kOutput, calls=%fused_computation.18 | convolution fusion | flops 2163212032 | bytes 13126664 | tf_op jit(solution)/shard_map/dot_general | solution.py:16
  119.5 0.0 copy-start.7
  119.5 2.0 copy-done.7
  121.5 7.7 %fusion.31 = f32[4096,1024]{1,0:T(8,128)} fusion(bf16[256,1024]{1,0:T(8,128)(2,1)S(1)} %reshape.130, f32[256,4096]{1,0:T(8,128)S(1)} %get-tuple-element.15, f32[4096]{0:T(1024)S(1)} %bitcast.21, f32[256]{0:T(256)S(1)} %reshape.169, s32[256]{0:T(256)S(1)} %iota_add_fusion, f32[]{:T(128)} %bitcast.1), kind=kOutput, calls=%fused_computation.68 | convolution fusion | flops 2160066560 | bytes 21514244 | tf_op jit(solution)/shard_map/dot_general | solution.py:101
  129.2 0.0 reduce-scatter.2.cloned.1.call-update
  129.2 0.8 div.14
  130.0 7.8 %all-to-all-start.5 = ((f32[128,1,2]{2,1,0:T(1,128)}), f32[128,1,2]{2,1,0:T(1,128)S(1)}, u32[]{:S(2)}, u32[]{:S(2)}) async-start(f32[128,1,2]{2,1,0:T(1,128)} %bitcast.4), calls=%async_computation.6 | async-start | bytes 131072 | tf_op jit(solution)/shard_map/all_to_all | solution.py:124
  137.8 8.6 %fusion.33 = f32[256,1024]{1,0:T(8,128)S(1)} fusion(bf16[4096,1024]{1,0:T(8,128)(2,1)} %all-gather.3.cloned.1.call-done, f32[256,4096]{1,0:T(8,128)} %copy-done.7, f32[4096]{0:T(1024)S(1)} %bitcast.22, f32[256]{0:T(256)S(1)} %reshape.169, s32[256]{0:T(256)S(1)} %iota_add_fusion, f32[]{:T(128)} %bitcast.1), kind=kOutput, calls=%fused_computation.69 | convolution fusion | flops 2160066560 | bytes 13649924 | tf_op jit(solution)/shard_map/dot_general | solution.py:99
  146.4 1.6 reshape.134
  148.0 0.0 all-to-all-done.5
  148.0 9.5 %all-to-all-start.3 = ((f32[128,2,1024]{2,1,0:T(2,128)}), f32[128,2,1024]{2,1,0:T(2,128)S(1)}, u32[]{:S(2)}, u32[]{:S(2)}) async-start(f32[128,2,1024]{2,1,0:T(2,128)} %reshape.134), calls=%async_computation.3 | async-start | bytes 2097152 | tf_op jit(solution)/shard_map/all_to_all | solution.py:110
  157.5 93.5 %reduce-scatter.2.cloned.1.call-done = f32[256,1024]{1,0:T(8,128)} async-done(((f32[4096,1024]{1,0:T(8,128)}), f32[256,1024]{1,0:T(8,128)}) %reduce-scatter.2.cloned.1.call-update) | async-done | bytes 1048592 | tf_op jit(solution)/shard_map/reduce_scatter | solution.py:100
  251.0 2.8 reshape.136
  253.8 0.0 all-to-all-done.3
  253.8 8.6 %all-to-all-start.4 = ((f32[128,2,1024]{2,1,0:T(2,128)}), f32[128,2,1024]{2,1,0:T(2,128)}, u32[]{:S(2)}, u32[]{:S(2)}) async-start(f32[128,2,1024]{2,1,0:T(2,128)} %reshape.136), calls=%async_computation.5 | async-start | bytes 2097152 | tf_op jit(solution)/shard_map/all_to_all | solution.py:117
  262.5 0.5 broadcast.97
  263.0 0.0 copy-done.6
  263.0 0.8 reduce.9
  263.9 0.1 reshape.138
  264.0 1.3 gather_fusion
  265.3 0.5 broadcast_select_fusion
  265.8 1.9 reshape.135
  267.7 1.6 gather_fusion.1
  269.3 11.7 %all-to-all-done.4 = f32[128,2,1024]{2,1,0:T(2,128)} async-done(((f32[128,2,1024]{2,1,0:T(2,128)}), f32[128,2,1024]{2,1,0:T(2,128)}, u32[]{:S(2)}, u32[]{:S(2)}) %all-to-all-start.4) | async-done | bytes 1048608 | tf_op jit(solution)/shard_map/all_to_all | solution.py:117
  281.0 1.9 reshape.137
  283.0 1.6 gather_fusion.2
  284.6 1.9 multiply_reduce_fusion
  286.5 2.8 fusion.11
  289.4 0.0 copy-done.1
  289.4 0.0 copy-done.5
  289.4 1.6 fusion.12
  (14 shorter events, 0.1 us)
Async XLA Ops:
  7.2 1.6 copy-start
  7.2 104.4 %all-gather.3.cloned.1.call-start = ((), (), s32[]{:S(2)}) async-start(), calls=%async_computation.7 | async-start | bytes 8912896 | tf_op jit(solution)/shard_map/all_gather | solution.py:93
  10.3 36.4 %copy-start.4 = (f32[128,1024]{1,0:T(8,128)}, f32[128,1024]{1,0:T(8,128)S(1)}, u32[]{:S(2)}) copy-start(f32[128,1024]{1,0:T(8,128)S(1)} %get-tuple-element.13) | copy-start | bytes 1572868
  12.7 0.8 copy-start.2
  42.2 13.9 %all-to-all-start.2 = ((bf16[128,1,2]{2,1,0:T(2,128)(2,1)}), bf16[128,1,2]{2,1,0:T(2,128)(2,1)S(1)}, u32[]{:S(2)}, u32[]{:S(2)}) async-start(bf16[128,1,2]{2,1,0:T(2,128)(2,1)} %all_to_all.29), calls=%async_computation.2 | async-start | bytes 131072 | tf_op jit(solution)/shard_map/all_to_all | solution.py:80
  56.0 26.7 %all-to-all-start = ((bf16[128,2,1024]{2,1,0:T(2,128)(2,1)}), bf16[128,2,1024]{2,1,0:T(2,128)(2,1)S(1)}, u32[]{:S(2)}, u32[]{:S(2)}) async-start(bf16[128,2,1024]{2,1,0:T(2,128)(2,1)} %reshape.129), calls=%async_computation | async-start | bytes 1048576 | tf_op jit(solution)/shard_map/all_to_all | solution.py:66
  60.5 190.5 %reduce-scatter.2.cloned.1.call-start = ((), (), s32[]{:S(2)}) async-start(), calls=%async_computation.8 | async-start | bytes 17825792 | tf_op jit(solution)/shard_map/reduce_scatter | solution.py:100
  119.5 2.0 copy-start.7
  130.0 18.0 %all-to-all-start.5 = ((f32[128,1,2]{2,1,0:T(1,128)}), f32[128,1,2]{2,1,0:T(1,128)S(1)}, u32[]{:S(2)}, u32[]{:S(2)}) async-start(f32[128,1,2]{2,1,0:T(1,128)} %bitcast.4), calls=%async_computation.6 | async-start | bytes 131072 | tf_op jit(solution)/shard_map/all_to_all | solution.py:124
  148.0 105.8 %all-to-all-start.3 = ((f32[128,2,1024]{2,1,0:T(2,128)}), f32[128,2,1024]{2,1,0:T(2,128)S(1)}, u32[]{:S(2)}, u32[]{:S(2)}) async-start(f32[128,2,1024]{2,1,0:T(2,128)} %reshape.134), calls=%async_computation.3 | async-start | bytes 2097152 | tf_op jit(solution)/shard_map/all_to_all | solution.py:110
  253.8 9.2 %copy-start.6 = (f32[128,2,1024]{2,1,0:T(2,128)}, f32[128,2,1024]{2,1,0:T(2,128)S(1)}, u32[]{:S(2)}) copy-start(f32[128,2,1024]{2,1,0:T(2,128)S(1)} %all-to-all-done.3) | copy-start | bytes 3145732
  253.8 27.2 %all-to-all-start.4 = ((f32[128,2,1024]{2,1,0:T(2,128)}), f32[128,2,1024]{2,1,0:T(2,128)}, u32[]{:S(2)}, u32[]{:S(2)}) async-start(f32[128,2,1024]{2,1,0:T(2,128)} %reshape.136), calls=%async_computation.5 | async-start | bytes 2097152 | tf_op jit(solution)/shard_map/all_to_all | solution.py:117
  284.6 4.8 %copy-start.1 = (bf16[1024,1024]{1,0:T(8,128)(2,1)S(1)}, bf16[1024,1024]{1,0:T(8,128)(2,1)}, u32[]{:S(2)}) copy-start(bf16[1024,1024]{1,0:T(8,128)(2,1)} %param.13) | copy-start | bytes 6291460
  284.6 4.8 %copy-start.3 = (f32[128,1024]{1,0:T(8,128)S(1)}, f32[128,1024]{1,0:T(8,128)}, u32[]{:S(2)}) copy-start(f32[128,1024]{1,0:T(8,128)} %copy-done.2) | copy-start | bytes 1572868
  284.6 4.8 %copy-start.5 = (f32[128,1024]{1,0:T(8,128)S(1)}, f32[128,1024]{1,0:T(8,128)}, u32[]{:S(2)}) copy-start(f32[128,1024]{1,0:T(8,128)} %gather_fusion.2) | copy-start | bytes 1572868
Sparse Core Ops, SparseCore 0:
  41.3 70.2 all-gather.2
  129.3 121.6 reduce-scatter.1
where the time goes:
time: 299 us; the launch traced here: 298 us
  waiting for transfers between devices  142 us (47%)
  blocking collectives  45.5 us (15%)
  starting transfers between devices  34.7 us (12%)
  matrix products  33.2 us (11%)
  local copies, waits for them, and re-layouts  21.4 us (7%)
  between operations  15.6 us (5%)
  other arithmetic  5.21 us (2%)
    reduce_scatter x1, waiting for transfers between devices, body(): lax.psum_scatter(lax.dot_general(weights, recv_img, (((0,), (0,)), ((), (...  93.5 us
    all_gather x1, waiting for transfers between devices, body(): lax.all_gather(recv_txt, 'blk', axis=0, tiled=True)  28.7 us
    all_to_all x1, blocking collectives, body(): lax.all_to_all(send_txt.reshape(devices, slot, width), ('grp', 'blk'), sp...  25.4 us
    all_gather x1, blocking collectives, body(): lax.all_gather(recv_live, 'blk', axis=0, tiled=True)  20.2 us
    all_to_all x1, waiting for transfers between devices, body(): lax.all_to_all(txt_grad.reshape(devices, slot, width), ('grp', 'blk'), sp...  11.7 us
    all_to_all x1, starting transfers between devices, body(): lax.all_to_all(img_grad.reshape(devices, slot, width), ('grp', 'blk'), sp...  9.51 us
    all_to_all x1, starting transfers between devices, body(): lax.all_to_all(txt_grad.reshape(devices, slot, width), ('grp', 'blk'), sp...  8.64 us
    dot_general x1, matrix products, body(): img_grad = jnp.dot(weights, texts_all, preferred_element_type=jnp.float32)  8.59 us
  transfers between devices with their start and end apart: 7, of which 4 were waited for; matrix products, arithmetic and copies ran while one was open for 8% of the time, Pallas kernels for 0%

commit v1 on v0

v1 whole, which is shorter than its diff:
```python
import functools

import jax
import jax.numpy as jnp
from jax import lax
from jax.experimental import pallas as pl
from jax.experimental.pallas import tpu as pltpu
from jax.sharding import PartitionSpec as P

EPS = 1e-06
CORES = 2
RING = 4
PEERS = 8
SLOTS = 32
HALF = SLOTS // 2
BLOCK = PEERS * SLOTS
EXTRA = 128
LEVELS = 32000.0
MESH = pl.DeviceIdType.MESH
F32 = jnp.float32
BF16 = jnp.bfloat16


def dot(a, b, da, db):
    return lax.dot_general(a, b, (((da,), (db,)), ((), ())), preferred_element_type=F32)


def encode(values, loss):
    rows = values.shape[0]
    top = jnp.max(jnp.abs(values), axis=1, keepdims=True)
    grade = jnp.ceil(8.0 * jnp.log2(jnp.maximum(top, 1e-30)))
    steps = jnp.round(values * (LEVELS * jnp.exp2(-0.125 * grade)))
    lane = lax.broadcasted_iota(jnp.int32, (rows, EXTRA), 1)
    extra = jnp.where(lane == 0, grade, 0.0)
    if loss is not None:
        loss_grade = jnp.ceil(8.0 * jnp.log2(jnp.maximum(loss, 1e-30)))
        scaled = loss * (LEVELS * jnp.exp2(-0.125 * loss_grade))
        high = jnp.round(scaled)
        low = jnp.round((scaled - high) * LEVELS)
        extra = jnp.where(lane == 1, loss_grade, extra)
        extra = jnp.where(lane == 2, high, extra)
        extra = jnp.where(lane == 3, low, extra)
    return steps.astype(jnp.int32).astype(jnp.int16), extra.astype(jnp.int32).astype(jnp.int16)


def decode(steps, extra, with_loss):
    values = steps * (jnp.exp2(0.125 * extra[:, 0:1]) * (1.0 / LEVELS))
    if not with_loss:
        return values, None
    scale = jnp.exp2(0.125 * extra[:, 1:2]) * (1.0 / LEVELS)
    return values, (extra[:, 2:3] + extra[:, 3:4] * (1.0 / LEVELS)) * scale


def kernel(
    scale_ref,
    bias_ref,
    img_feats,
    txt_feats,
    img_head,
    txt_head,
    ids,
    placement,
    out_img,
    out_txt,
    out_loss,
    layout,
    unit,
    factor,
    pack,
    held,
    live,
    coef,
    losses,
    part,
    away,
    near,
    far,
    back,
    sa,
    ra,
    sg,
    rg,
    sl,
    rl,
    s1,
    r1,
    s2,
    r2,
    sb,
    rb,
):
    width = img_head.shape[1]
    pairs = img_feats.shape[0]
    g = lax.axis_index("grp")
    b = lax.axis_index("blk")
    x, core = lax.div(g, CORES), lax.rem(g, CORES)
    y, z = lax.div(b, RING), lax.rem(b, RING)

    def peer(k):
        dx, dc = lax.div(k, CORES), lax.rem(k, CORES)
        return (lax.rem(x + dx, RING) * CORES + lax.rem(core + dc, CORES), b)

    def facing(k):
        dx, dc = lax.div(k, CORES), lax.rem(k, CORES)
        return lax.rem(RING - dx, RING) * CORES + dc

    def neighbour(kind, side):
        step = 1 if side == 0 else RING - 1
        if kind == 0:
            return (g, y * RING + lax.rem(z + step, RING))
        return (g, lax.rem(y + step, RING) * RING + z)

    def copy(src, dst, send, recv, device):
        return pltpu.make_async_remote_copy(
            src_ref=src,
            dst_ref=dst,
            send_sem=send,
            recv_sem=recv,
            device_id=device,
            device_id_type=MESH,
        )

    def chunk(k):
        return pl.ds(pl.multiple_of(k * SLOTS, SLOTS), SLOTS)

    barrier = pltpu.get_barrier_semaphore()

    @pl.loop(1, PEERS)
    def _(k):
        pl.semaphore_signal(barrier, inc=1, device_id=peer(k), device_id_type=MESH)

    for kind in range(2):
        for side in range(2):
            pl.semaphore_signal(
                barrier, inc=1, device_id=neighbour(kind, side), device_id_type=MESH
            )

    lane = lax.broadcasted_iota(jnp.int32, (pairs, 128), 1)
    row = lax.broadcasted_iota(jnp.int32, (pairs, 128), 0)
    place = placement[...].astype(F32)
    target = jnp.sum(jnp.where(ids[...] == lane, place, 0.0), axis=1, keepdims=True)
    team = jnp.floor(target * (1.0 / (RING * RING)))
    team_x = jnp.floor(team * (1.0 / CORES))
    dx = team_x - x.astype(F32)
    dc = team - CORES * team_x - core.astype(F32)
    where_to = CORES * jnp.where(dx < 0, dx + RING, dx) + jnp.where(dc < 0, dc + CORES, dc)
    chosen = jnp.where(where_to == lane.astype(F32), 1.0, 0.0)
    before = jnp.where(row > lane, 1.0, 0.0).astype(BF16)
    earlier = dot(before, chosen.astype(BF16), 1, 0)
    rank = jnp.sum(earlier * chosen, axis=1, keepdims=True)
    slot = where_to * SLOTS + rank
    slots = lax.broadcasted_iota(jnp.int32, (pairs, BLOCK), 1).astype(F32)
    layout[...] = jnp.where(slots == slot, 1.0, 0.0).astype(BF16)

    filled = dot(layout[...], jnp.ones((pairs, 128), BF16), 0, 0)
    lane_block = lax.broadcasted_iota(jnp.int32, (BLOCK, 128), 1)
    mark = jnp.where(lane_block == 0, 2.0 - 2.0 * filled, 0.0)

    pl.semaphore_wait(barrier, PEERS - 1 + 4)

    for kind, feats, head in ((0, img_feats, img_head), (1, txt_feats, txt_head)):
        raw = dot(feats[...], head[...], 1, 0)
        scale_back = lax.rsqrt(jnp.sum(raw * raw, axis=1, keepdims=True) + EPS)
        unit[kind] = raw * scale_back
        factor[kind] = jnp.broadcast_to(scale_back, (pairs, 128))
        rows = dot(layout[...], unit[kind].astype(BF16), 0, 0)
        pack[kind, :, 128:] = rows[:, 128:].astype(BF16)
        pack[kind, :, :128] = (rows[:, :128] + mark).astype(BF16)

        @pl.loop(1, PEERS)
        def _(k):
            copy(
                pack.at[kind, chunk(k)],
                held.at[kind, 0, chunk(facing(k))],
                sa.at[kind, k],
                ra.at[kind, facing(k)],
                peer(k),
            ).start()

        held[kind, 0, :SLOTS] = pack[kind, :SLOTS]

    def gathered(kind, side, k):
        return copy(
            held.at[kind, 0, chunk(k)],
            held.at[kind, 3 if side == 0 else 1, chunk(k)],
            sg.at[kind, side, k],
            rg.at[kind, side, k],
            neighbour(kind, side),
        )

    def passed(kind, side, k):
        rows = pl.ds(pl.multiple_of(k * SLOTS + side * HALF, HALF), HALF)
        return copy(
            held.at[kind, 3 if side == 0 else 1, rows],
            held.at[kind, 2, rows],
            sl.at[kind, side, k],
            rl.at[kind, side, k],
            neighbour(kind, side),
        )

    def arrived(kind, k):
        return copy(
            pack.at[kind, chunk(k)],
            held.at[kind, 0, chunk(k)],
            sa.at[kind, k],
            ra.at[kind, k],
            peer(k),
        )

    for kind in range(2):
        for side in range(2):
            gathered(kind, side, 0).start()

    @pl.loop(1, PEERS)
    def _(k):
        for kind in range(2):
            arrived(kind, k).wait_recv()
            for side in range(2):
                gathered(kind, side, k).start()

    @pl.loop(0, PEERS)
    def _(k):
        for kind in range(2):
            for side in range(2):
                gathered(kind, side, k).wait_recv()
                passed(kind, side, k).start()

    @pl.loop(0, PEERS)
    def _(k):
        for kind in range(2):
            for side in range(2):
                passed(kind, side, k).wait_recv()

    scale_t = jnp.exp(jnp.full((1, BLOCK), scale_ref[0], F32))
    shift = bias_ref[0]
    first_lane = jnp.where(lax.broadcasted_iota(jnp.int32, (8, 128), 1) == 0, 1.0, 0.0)
    for j in range(RING):
        heads_of = dot(first_lane.astype(BF16), held[1, j, :, :128], 1, 1)
        live[j] = jnp.where(heads_of < 1.5, 1.0, 0.0)
    losses[...] = jnp.zeros_like(losses)
    same = lax.broadcasted_iota(jnp.int32, (BLOCK, BLOCK), 0) == lax.broadcasted_iota(
        jnp.int32, (BLOCK, BLOCK), 1
    )

    @pl.loop(0, RING * RING)
    def _(t):
        i, j = lax.div(t, RING), lax.rem(t, RING)
        images = held[0, i]
        sims = dot(images, held[1, j], 1, 1)
        own = jnp.where(t == 0, 1.0, 0.0)
        sign = jnp.where(same, 1.0 - 2.0 * own, 1.0)
        logits = sign * (scale_t * sims + shift)
        small = jnp.exp(-jnp.abs(logits))
        whole = 1.0 + small
        inverse = 1.0 / whole
        image_live = jnp.where(images[:, 0:1].astype(F32) < 1.5, 1.0, 0.0)
        text_live = live[j][0:1]
        log_term = jnp.log(whole) + (small - (whole - 1.0)) * inverse
        terms = (jnp.maximum(logits, 0.0) + log_term) * text_live
        losses[i] += terms[:, :128] + terms[:, 128:]
        rate = jnp.where(logits >= 0, inverse, small * inverse)
        weights = (sign * scale_t) * rate * (image_live * text_live)
        coef[
            pl.ds(pl.multiple_of(i * BLOCK, BLOCK), BLOCK),
            pl.ds(pl.multiple_of(j * BLOCK, BLOCK), BLOCK),
        ] = weights.astype(BF16)

    def terms_of(kind, n):
        @pl.loop(0, width // 256)
        def _(q):
            lanes = pl.ds(pl.multiple_of(q * 256, 256), 256)
            total = jnp.zeros((BLOCK, 256), F32)
            for j in range(RING):
                if kind == 0:
                    total += dot(
                        coef[n * BLOCK : (n + 1) * BLOCK, j * BLOCK : (j + 1) * BLOCK],
                        held[1, j, :, lanes],
                        1,
                        0,
                    )
                else:
                    total += dot(
                        coef[j * BLOCK : (j + 1) * BLOCK, n * BLOCK : (n + 1) * BLOCK],
                        held[0, j, :, lanes],
                        0,
                        0,
                    )
            part[kind, n, :, lanes] = total

    def loss_of(n, k):
        return jnp.sum(losses[n, chunk(k)], axis=1, keepdims=True)

    def store(kind, n, k, values, loss):
        steps, extra = encode(values, loss)
        away[kind, n, chunk(k), :width] = steps
        away[kind, n, chunk(k), width:] = extra

    def load(ref):
        value = ref[...].astype(F32)
        return value[:, :width], value[:, width:]

    def first(kind, side, k):
        rows = pl.ds(pl.multiple_of(k * SLOTS + side * HALF, HALF), HALF)
        return copy(
            away.at[kind, 2, rows],
            far.at[kind, side, k],
            s1.at[kind, side, k],
            r1.at[kind, side, k],
            neighbour(kind, side),
        )

    def second(kind, side, k):
        return copy(
            away.at[kind, 1 if side == 0 else 3, chunk(k)],
            near.at[kind, side, chunk(k)],
            s2.at[kind, side, k],
            r2.at[kind, side, k],
            neighbour(kind, side),
        )

    def last(kind, k):
        return copy(
            away.at[kind, 0, chunk(k)],
            back.at[kind, chunk(facing(k))],
            sb.at[kind, k],
            rb.at[kind, facing(k)],
            peer(k),
        )

    def returned(kind, k):
        return copy(
            away.at[kind, 0, chunk(k)],
            back.at[kind, chunk(k)],
            sb.at[kind, k],
            rb.at[kind, k],
            peer(k),
        )

    for kind in range(2):
        terms_of(kind, 2)

        @pl.loop(0, PEERS)
        def _(k):
            store(kind, 2, k, part[kind, 2, chunk(k)], loss_of(2, k) if kind == 0 else None)
            first(kind, 0, k).start()
            first(kind, 1, k).start()

    for kind in range(2):
        for n in (1, 3, 0):
            terms_of(kind, n)

    for kind in range(2):
        for side in range(2):
            n = 1 if side == 0 else 3

            @pl.loop(0, PEERS)
            def _(k):
                first(kind, side, k).wait_recv()
                steps, extra = load(far.at[kind, side, k])
                values, loss = decode(steps, extra, kind == 0)
                mine = part[kind, n, chunk(k)]
                pad = jnp.zeros((HALF, width), F32)
                order = [values, pad] if side == 0 else [pad, values]
                mine += jnp.concatenate(order, axis=0)
                loss_mine = None
                if kind == 0:
                    pad = jnp.zeros((HALF, 1), F32)
                    order = [loss, pad] if side == 0 else [pad, loss]
                    loss_mine = loss_of(n, k) + jnp.concatenate(order, axis=0)
                store(kind, n, k, mine, loss_mine)
                second(kind, side, k).start()

    for kind in range(2):

        def finish(k):
            mine = part[kind, 0, chunk(k)]
            loss_mine = loss_of(0, k) if kind == 0 else None
            for side in range(2):
                second(kind, side, k).wait_recv()
                steps, extra = load(near.at[kind, side, chunk(k)])
                values, loss = decode(steps, extra, kind == 0)
                mine += values
                if kind == 0:
                    loss_mine += loss
            store(kind, 0, k, mine, loss_mine)

        @pl.loop(1, PEERS)
        def _(k):
            finish(k)
            last(kind, k).start()

        finish(0)
        back[kind, :SLOTS] = away[kind, 0, :SLOTS]

    for kind, head, out in ((0, img_head, out_img), (1, txt_head, out_txt)):

        @pl.loop(1, PEERS)
        def _(k):
            returned(kind, k).wait_recv()

        steps = back[kind].astype(jnp.int32)
        high = lax.shift_right_arithmetic(steps, 8)
        low = steps - lax.shift_left(high, 8)
        high = dot(layout[...], high.astype(F32).astype(BF16), 1, 0)
        low = dot(layout[...], low.astype(F32).astype(BF16), 1, 0)
        own = high * 256.0 + low
        grad, loss = decode(own[:, :width], own[:, width:], kind == 0)
        if kind == 0:
            loss = jnp.broadcast_to(loss * (1.0 / (RING * RING * pairs)), (pairs, 128))
            out_loss[...] = jnp.transpose(loss)[0:8]
        along = jnp.sum(unit[kind] * grad, axis=1, keepdims=True)
        local = ((grad - unit[kind] * along) * factor[kind][:, 0:1]).astype(BF16)
        out[...] = dot(local, head[...], 1, 1)

    @pl.loop(1, PEERS)
    def _(k):
        for kind in range(2):
            arrived(kind, k).wait_send()
            last(kind, k).wait_send()

    @pl.loop(0, PEERS)
    def _(k):
        for kind in range(2):
            for side in range(2):
                gathered(kind, side, k).wait_send()
                passed(kind, side, k).wait_send()
                first(kind, side, k).wait_send()
                second(kind, side, k).wait_send()


def body(img_feats, txt_feats, img_head, txt_head, cluster_ids, placement, log_scale, bias):
    pairs, width = img_feats.shape[0], img_head.shape[1]
    wide = width + EXTRA
    dma = pltpu.SemaphoreType.DMA
    vmem, smem = pl.BlockSpec(memory_space=pltpu.VMEM), pl.BlockSpec(memory_space=pltpu.SMEM)
    img, txt, loss = pl.pallas_call(
        kernel,
        out_shape=(
            jax.ShapeDtypeStruct((pairs, width), F32),
            jax.ShapeDtypeStruct((pairs, width), F32),
            jax.ShapeDtypeStruct((8, pairs), F32),
        ),
        in_specs=[smem, smem] + [vmem] * 6,
        out_specs=(vmem, vmem, vmem),
        scratch_shapes=[
            pltpu.VMEM((pairs, BLOCK), BF16),
            pltpu.VMEM((2, pairs, width), F32),
            pltpu.VMEM((2, pairs, 128), F32),
            pltpu.VMEM((2, BLOCK, width), BF16),
            pltpu.VMEM((2, RING, BLOCK, width), BF16),
            pltpu.VMEM((RING, 8, BLOCK), F32),
            pltpu.VMEM((RING * BLOCK, RING * BLOCK), BF16),
            pltpu.VMEM((RING, BLOCK, 128), F32),
            pltpu.VMEM((2, RING, BLOCK, width), F32),
            pltpu.VMEM((2, RING, BLOCK, wide), jnp.int16),
            pltpu.VMEM((2, 2, BLOCK, wide), jnp.int16),
            pltpu.VMEM((2, 2, PEERS, HALF, wide), jnp.int16),
            pltpu.VMEM((2, BLOCK, wide), jnp.int16),
            dma((2, PEERS)),
            dma((2, PEERS)),
            dma((2, 2, PEERS)),
            dma((2, 2, PEERS)),
            dma((2, 2, PEERS)),
            dma((2, 2, PEERS)),
            dma((2, 2, PEERS)),
            dma((2, 2, PEERS)),
            dma((2, 2, PEERS)),
            dma((2, 2, PEERS)),
            dma((2, PEERS)),
            dma((2, PEERS)),
        ],
        compiler_params=pltpu.CompilerParams(
            collective_id=0, has_side_effects=True, vmem_limit_bytes=56 * 1024 * 1024
        ),
    )(
        log_scale,
        bias,
        img_feats,
        txt_feats,
        img_head,
        txt_head,
        cluster_ids,
        placement.reshape(1, -1),
    )
    return img, txt, loss[0]


def solution(mesh):
    placed = (
        P(("grp", "blk"), None),
        P(("grp", "blk"), None),
        P(),
        P(),
        P(("grp", "blk"), None),
        P(),
        P(),
        P(),
    )
    return jax.shard_map(
        body,
        mesh=mesh,
        in_specs=placed,
        out_specs=(P(("grp", "blk"), None), P(("grp", "blk"), None), P(("grp", "blk"))),
        check_vma=False,
    )
```

time: 299 us -> 99.9 us (0.33)
  waiting for transfers between devices: 142 us -> 0 us
  Pallas kernels: 0 us -> 91.3 us
  blocking collectives: 45.5 us -> 0 us
  starting transfers between devices: 34.7 us -> 0 us
  matrix products: 33.2 us -> 0 us
  local copies, waits for them, and re-layouts: 21.4 us -> 6.35 us
  between operations: 15.6 us -> 1.93 us
  other arithmetic: 5.21 us -> 0 us
    reduce_scatter x1 -> x0, waiting for transfers between devices: 93.5 us -> none  [body(): lax.psum_scatter(lax.dot_general(weights, recv_img, (((0,), (0,)), ((), (...]
    pallas_call x0 -> x1, Pallas kernels: none -> 91.3 us  [body(): pl.pallas_call(kernel, out_shape=(jax.ShapeDtypeStruct((pairs, width), F3...]
    all_to_all x5 -> x0, starting transfers between devices: 34.6 us -> none  [the longest x1 9.51 us: body(): lax.all_to_all(img_grad.reshape(devices, slot, width), ('grp', 'blk'), sp...]
    dot_general x9 -> x0, matrix products: 33.2 us -> none  [the longest x1 8.59 us: body(): img_grad = jnp.dot(weights, texts_all, preferred_element_type=jnp.float32)]
    all_gather x1 -> x0, waiting for transfers between devices: 28.7 us -> none  [body(): lax.all_gather(recv_txt, 'blk', axis=0, tiled=True)]
    all_to_all x1 -> x0, blocking collectives: 25.4 us -> none  [body(): lax.all_to_all(send_txt.reshape(devices, slot, width), ('grp', 'blk'), sp...]
    all_gather x1 -> x0, blocking collectives: 20.2 us -> none  [body(): lax.all_gather(recv_live, 'blk', axis=0, tiled=True)]
    all_to_all x5 -> x0, waiting for transfers between devices: 20.1 us -> none  [the longest x1 11.7 us: body(): lax.all_to_all(txt_grad.reshape(devices, slot, width), ('grp', 'blk'), sp...]
  transfers between devices with their start and end apart: 7 -> 0, of which waited for: 4 -> 0; matrix products, arithmetic and copies ran while one was open for 8% -> 0% of each run, Pallas kernels for 0% -> 0%
where the time goes in v1:
time: 99.9 us; the launch traced here: 99.6 us
  Pallas kernels  91.3 us (91%)
  local copies, waits for them, and re-layouts  6.35 us (6%)
  between operations  1.93 us (2%)
    pallas_call x1, Pallas kernels, body(): pl.pallas_call(kernel, out_shape=(jax.ShapeDtypeStruct((pairs, width), F3...  91.3 us
    unnamed x3, local copies, waits for them, and re-layouts  5.16 us

profile of v1, /device:TPU:1, one launch (start us, length us, event | category | flops | bytes accessed | tf_op | source)
XLA Modules:
  0.0 99.6 jit_solution(8675344151073377981)
XLA Ops:
  1.9 1.4 %copy.11.ids = s32[128,1]{1,0:T(8,128)} copy(s32[128,1]{0,1:T(1,128)} %param.12) | data formatting | bytes 1024 | tf_op args[4]
  3.3 91.3 %shard_map.103 = (f32[128,1024]{1,0:T(8,128)}, f32[128,1024]{1,0:T(8,128)}, f32[8,128]{1,0:T(8,128)}) custom-call(f32[1]{0:T(128)S(6)} %copy.14.scale_ref, f32[1]{0:T(128)S(6)} %copy.15.bias_ref, bf16[128,1024]{1,0:T(8,128)(2,1)} %img_feats.1, bf16[128,1024]{1,0:T(8,128)(2,1)} %txt_feats.1, bf16[1024,1024]{1,0:T(8,128)(2,1)} %img_head.1, ...), custom_call_target="tpu_custom_call" | custom-call | tf_op jit(solution)/shard_map/pallas_call | solution.py:436
  94.7 1.2 %slice_bitcast_fusion = f32[128]{0:T(128)} fusion(f32[8,128]{1,0:T(8,128)} %get-tuple-element.8), kind=kLoop, calls=%fused_computation | loop fusion | bytes 1024 | tf_op jit(solution)/shard_map/squeeze | solution.py:485
  95.9 1.9 %copy.16 = f32[128,1024]{1,0:T(8,128)} copy(f32[128,1024]{1,0:T(8,128)} %get-tuple-element.12) | data formatting | bytes 1048576
  97.7 1.9 %copy.17 = f32[128,1024]{1,0:T(8,128)} copy(f32[128,1024]{1,0:T(8,128)} %get-tuple-element.13) | data formatting | bytes 1048576

commit v2 on v1

v2 whole, which is shorter than its diff:
```python
import functools

import jax
import jax.numpy as jnp
from jax import lax
from jax.experimental import pallas as pl
from jax.experimental.pallas import tpu as pltpu
from jax.sharding import PartitionSpec as P

EPS = 1e-06
CORES = 2
RING = 4
PEERS = 8
MOST = 32
TILE = 256
EXTRA = 128
LEVELS = 32000.0
AROUND = (0, 1, 3, 2)
FACING = (0, 2, 1, 3)
OWN, NEXT, PREV, FAR = range(4)
MESH = pl.DeviceIdType.MESH
F32 = jnp.float32
BF16 = jnp.bfloat16
LOG2E = 1.4426950408889634


def dot(a, b, da, db):
    return lax.dot_general(a, b, (((da,), (db,)), ((), ())), preferred_element_type=F32)


def encode(values, loss, alarm):
    rows = values.shape[0]
    top = jnp.max(jnp.abs(values), axis=1, keepdims=True)
    grade = jnp.ceil(8.0 * jnp.log2(jnp.maximum(top, 1e-30)))
    steps = jnp.round(values * (LEVELS * jnp.exp2(-0.125 * grade)))
    lane = lax.broadcasted_iota(jnp.int32, (rows, EXTRA), 1)
    extra = jnp.where(lane == 0, grade, 0.0)
    if loss is not None:
        loss_grade = jnp.ceil(8.0 * jnp.log2(jnp.maximum(loss, 1e-30)))
        scaled = loss * (LEVELS * jnp.exp2(-0.125 * loss_grade))
        high = jnp.round(scaled)
        low = jnp.round((scaled - high) * LEVELS)
        extra = jnp.where(lane == 1, loss_grade, extra)
        extra = jnp.where(lane == 2, high, extra)
        extra = jnp.where(lane == 3, low, extra)
        extra = jnp.where(lane == 4, alarm, extra)
    return steps, extra


def decode(coded, width, with_loss):
    extra = coded[:, width:]
    values = coded[:, :width] * (jnp.exp2(0.125 * extra[:, 0:1]) * (1.0 / LEVELS))
    if not with_loss:
        return values, None, None
    scale = jnp.exp2(0.125 * extra[:, 1:2]) * (1.0 / LEVELS)
    loss = (extra[:, 2:3] + extra[:, 3:4] * (1.0 / LEVELS)) * scale
    return values, loss, extra[:, 4:5]


def kernel(
    slots,
    scale_ref,
    bias_ref,
    img_feats,
    txt_feats,
    img_head,
    txt_head,
    ids,
    placement,
    out_img,
    out_txt,
    out_loss,
    out_alarm,
    feats,
    head,
    layout,
    unit,
    factor,
    pack,
    held,
    coef,
    turned,
    losses,
    part,
    away,
    near,
    far,
    back,
    si,
    sa,
    ra,
    sg,
    rg,
    sl,
    rl,
    s1,
    r1,
    s2,
    r2,
    sb,
    rb,
):
    width = img_head.shape[1]
    pairs = img_feats.shape[0]
    groups = slots // 8
    block = PEERS * groups
    block_rows = PEERS * slots
    early = 3 * block_rows // TILE
    g = lax.axis_index("grp")
    b = lax.axis_index("blk")
    x, core = lax.div(g, CORES), lax.rem(g, CORES)
    y, z = lax.div(b, RING), lax.rem(b, RING)

    def peer(k):
        to_x = lax.rem(x + AROUND[k // CORES], RING)
        return (to_x * CORES + lax.rem(core + k % CORES, CORES), b)

    def facing(k):
        return FACING[k // CORES] * CORES + k % CORES

    def neighbour(kind, side):
        step = 1 if side == 0 else RING - 1
        if kind == 0:
            return (g, y * RING + lax.rem(z + step, RING))
        return (g, lax.rem(y + step, RING) * RING + z)

    def copy(src, dst, send, recv, device):
        return pltpu.make_async_remote_copy(
            src_ref=src,
            dst_ref=dst,
            send_sem=send,
            recv_sem=recv,
            device_id=device,
            device_id_type=MESH,
        )

    def chunk(k, at=0):
        return pl.ds(at * block + k * groups, groups)

    loads = []
    for n, (src, dst) in enumerate(
        (
            (img_feats, feats.at[0]),
            (img_head, head.at[0]),
            (txt_feats, feats.at[1]),
            (txt_head, head.at[1]),
        )
    ):
        loads.append(pltpu.make_async_copy(src, dst, si.at[n]))
        loads[-1].start()

    barrier = pltpu.get_barrier_semaphore()
    for k in range(1, PEERS):
        pl.semaphore_signal(barrier, inc=1, device_id=peer(k), device_id_type=MESH)
    for kind in range(2):
        for side in range(2):
            pl.semaphore_signal(
                barrier, inc=1, device_id=neighbour(kind, side), device_id_type=MESH
            )

    lane = lax.broadcasted_iota(jnp.int32, (pairs, 128), 1)
    row = lax.broadcasted_iota(jnp.int32, (pairs, 128), 0)
    lane_f = lane.astype(F32)
    place = placement[...].astype(F32)
    named = jnp.transpose(jnp.broadcast_to(ids[...].astype(F32), (pairs, pairs)))
    target = jnp.sum(jnp.where(named == lane_f, place, 0.0), axis=1, keepdims=True)
    team = jnp.floor(target * (1.0 / (RING * RING)))
    team_x = jnp.floor(team * (1.0 / CORES))
    dx = team_x - x.astype(F32)
    dx = jnp.where(dx < 0, dx + RING, dx)
    dx = jnp.where(dx == 2, 3.0, jnp.where(dx == 3, 2.0, dx))
    dc = team - CORES * team_x - core.astype(F32)
    where_to = CORES * dx + jnp.where(dc < 0, dc + CORES, dc)
    chosen = jnp.where(where_to == lane_f, 1.0, 0.0)
    before = jnp.where(row > lane, 1.0, 0.0).astype(BF16)
    earlier = dot(before, chosen.astype(BF16), 1, 0)
    rank = jnp.sum(earlier * chosen, axis=1, keepdims=True)
    slot = jnp.where(rank < slots, where_to * slots + rank, -1.0)
    spots = lax.broadcasted_iota(jnp.int32, (pairs, TILE), 1).astype(F32)
    layout[...] = jnp.where(spots == slot, 1.0, 0.0).astype(BF16)

    crowded = jnp.where(jnp.max(rank, axis=0, keepdims=True) >= slots, 4.0, 0.0)
    filled = dot(layout[...], jnp.ones((pairs, 128), BF16), 0, 0)[:block_rows]
    lane_block = lax.broadcasted_iota(jnp.int32, (block_rows, 128), 1)
    row_block = lax.broadcasted_iota(jnp.int32, (block_rows, 128), 0)
    mark = 2.0 - 2.0 * filled
    if slots < MOST:
        mark += jnp.where(lax.rem(row_block, slots) == 0, crowded, 0.0)
    mark = jnp.where(lane_block == 0, mark, 0.0)

    def arrived(kind, k):
        return copy(
            pack.at[kind, chunk(k)],
            held.at[kind, chunk(k)],
            sa.at[kind, k],
            ra.at[kind, k],
            peer(k),
        )

    def gathered(kind, side, k):
        return copy(
            held.at[kind, chunk(k)],
            held.at[kind, chunk(k, PREV if side == 0 else NEXT)],
            sg.at[kind, side, k],
            rg.at[kind, side, k],
            neighbour(kind, side),
        )

    def passed(kind, k):
        side = k % 2
        return copy(
            held.at[kind, chunk(k, PREV if side == 0 else NEXT)],
            held.at[kind, chunk(k, FAR)],
            sl.at[kind, k],
            rl.at[kind, k],
            neighbour(kind, side),
        )

    for kind in range(2):
        loads[2 * kind].wait()
        loads[2 * kind + 1].wait()
        raw = dot(feats[kind], head[kind], 1, 0)
        scale_back = lax.rsqrt(jnp.sum(raw * raw, axis=1, keepdims=True) + EPS)
        unit[kind] = raw * scale_back
        factor[kind] = jnp.broadcast_to(scale_back, (pairs, 128))
        rows = dot(layout[...], unit[kind].astype(BF16), 0, 0)[:block_rows]
        first = (rows[:, :128] + mark).reshape(block, 8, 128)
        pack[kind, :, :, :128] = first.astype(BF16)
        pack[kind, :, :, 128:] = rows[:, 128:].reshape(block, 8, width - 128).astype(BF16)
        held[kind, :groups] = pack[kind, :groups]
        if kind == 0:
            pl.semaphore_wait(barrier, PEERS - 1 + 4)
        for k in range(1, PEERS):
            copy(
                pack.at[kind, chunk(k)],
                held.at[kind, chunk(facing(k))],
                sa.at[kind, k],
                ra.at[kind, facing(k)],
                peer(k),
            ).start()
        for side in range(2):
            gathered(kind, side, 0).start()

    def pass_on(k):
        for kind in range(2):
            gathered(kind, k % 2, k).wait_recv()
            passed(kind, k).start()

    for k in range(1, PEERS):
        for kind in range(2):
            arrived(kind, k).wait_recv()
            for side in range(2):
                gathered(kind, side, k).start()
        pass_on(k - 1)
    pass_on(PEERS - 1)
    for k in range(PEERS):
        for kind in range(2):
            gathered(kind, 1 - k % 2, k).wait_recv()

    scale_t = jnp.exp(jnp.full((1, 1), scale_ref[0], F32))
    shift = bias_ref[0]
    first_lane = jnp.where(lax.broadcasted_iota(jnp.int32, (8, 128), 1) == 0, 1.0, 0.0)
    losses[...] = jnp.zeros_like(losses)

    def tile_of(i, j, with_own):
        span = TILE // 8
        images = held[0, pl.ds(i * span, span)].reshape(TILE, width)
        texts = held[1, pl.ds(j * span, span)].reshape(TILE, width)
        sims = dot(images, texts, 1, 1)
        text_first = dot(first_lane.astype(BF16), texts[:, :128], 1, 1)[0:1]
        base = jnp.where(text_first < 1.5, shift * LOG2E, -1e5)
        powers = sims * (scale_t * LOG2E) + base
        if with_own:
            row = lax.broadcasted_iota(jnp.int32, (TILE, TILE), 0)
            same = row == lax.broadcasted_iota(jnp.int32, (TILE, TILE), 1)
            same = jnp.logical_and(same, row < block_rows)
            same = jnp.logical_and(same, powers > -5e4)
            powers = jnp.where(same, -powers, powers)
        odds = jnp.exp2(powers)
        whole = 1.0 + odds
        inverse = 1.0 / whole
        terms = jnp.log(whole) + (odds - (whole - 1.0)) * inverse
        rows = pl.ds(pl.multiple_of(i * TILE, TILE), TILE)
        columns = pl.ds(pl.multiple_of(j * TILE, TILE), TILE)
        losses[rows] += terms[:, :128] + terms[:, 128:]
        weights = odds * inverse * jnp.where(images[:, 0:1].astype(F32) < 1.5, scale_t, 0.0)
        if with_own:
            weights = jnp.where(same, -weights, weights)
        coef[rows, columns] = weights.astype(BF16)
        turned[columns, rows] = jnp.transpose(weights).astype(BF16)

    tile_of(0, 0, True)

    @pl.loop(1, early * early)
    def _(t):
        tile_of(lax.div(t, early), lax.rem(t, early), False)

    for k in range(PEERS):
        for kind in range(2):
            passed(kind, k).wait_recv()

    @pl.loop(0, early)
    def _(t):
        tile_of(t, early, False)

    @pl.loop(0, early + 1)
    def _(t):
        tile_of(early, t, False)

    alarm = None
    if slots < MOST:
        starts = jnp.zeros((8, 128), F32)
        for kind in range(2):
            starts = jnp.maximum(starts, jnp.max(held[kind, :, :, :128].astype(F32), axis=0))
        starts = jnp.where(lax.broadcasted_iota(jnp.int32, (8, 128), 1) == 0, starts, 0.0)
        starts = jnp.max(jnp.max(starts, axis=1, keepdims=True), axis=0, keepdims=True)
        alarm = jnp.where(starts > 2.5, 1.0, 0.0)
    else:
        alarm = jnp.zeros((1, 1), F32)

    def terms_of(kind, start, size):
        weights = coef if kind == 0 else turned

        @pl.loop(0, width // TILE)
        def _(q):
            lanes = pl.ds(pl.multiple_of(q * TILE, TILE), TILE)
            others = held[1 - kind, :, :, lanes].reshape(RING * block_rows, TILE)
            rows = pl.ds(start * block_rows, size * block_rows)
            part[kind, rows, lanes] = dot(weights[rows], others, 1, 0)

    def at(n, k):
        return pl.ds(n * block_rows + k * slots, slots)

    def loss_of(n, k):
        return jnp.sum(losses[at(n, k)], axis=1, keepdims=True)

    def store(kind, n, k, values, loss, alarm):
        steps, extra = encode(values, loss, alarm)
        steps = steps.reshape(groups, 8, width).astype(jnp.int32)
        away[kind, n, chunk(k), :, :width] = steps.astype(jnp.int16)
        extra = extra.reshape(groups, 8, EXTRA).astype(jnp.int32)
        away[kind, n, chunk(k), :, width:] = extra.astype(jnp.int16)

    def load(ref, kind):
        value = ref[...].astype(F32).reshape(slots, width + EXTRA)
        return decode(value, width, kind == 0)

    def first(kind, k):
        return copy(
            away.at[kind, FAR, chunk(k)],
            far.at[kind, chunk(k)],
            s1.at[kind, k],
            r1.at[kind, k],
            neighbour(kind, k % 2),
        )

    def second(kind, side, k):
        return copy(
            away.at[kind, NEXT if side == 0 else PREV, chunk(k)],
            near.at[kind, side, chunk(k)],
            s2.at[kind, side, k],
            r2.at[kind, side, k],
            neighbour(kind, side),
        )

    def returned(kind, k):
        return copy(
            away.at[kind, OWN, chunk(k)],
            back.at[kind, chunk(k)],
            sb.at[kind, k],
            rb.at[kind, k],
            peer(k),
        )

    order = tuple(range(PEERS - 1, -1, -1))
    for kind in range(2):
        terms_of(kind, FAR, 1)
        for k in order:
            values = part[kind, at(FAR, k)]
            store(kind, FAR, k, values, loss_of(FAR, k) if kind == 0 else None, alarm)
            first(kind, k).start()

    for kind in range(2):
        terms_of(kind, NEXT, 2)
        for k in order:
            n = PREV if k % 2 == 0 else NEXT
            values = part[kind, at(n, k)]
            store(kind, n, k, values, loss_of(n, k) if kind == 0 else None, alarm)
            second(kind, 1 - k % 2, k).start()

    for kind in range(2):
        terms_of(kind, OWN, 1)

    for k in order:
        n = NEXT if k % 2 == 0 else PREV
        for kind in range(2):
            first(kind, k).wait_recv()
        for kind in range(2):
            values, loss, alarms = load(far.at[kind, chunk(k)], kind)
            values += part[kind, at(n, k)]
            if kind == 0:
                loss += loss_of(n, k)
                alarms = jnp.maximum(alarms, alarm)
            store(kind, n, k, values, loss, alarms)
        for kind in range(2):
            second(kind, k % 2, k).start()

    for k in order:
        for kind in range(2):
            for side in range(2):
                second(kind, side, k).wait_recv()
        for kind in range(2):
            values = part[kind, at(OWN, k)]
            loss, alarms = None, None
            if kind == 0:
                loss, alarms = loss_of(OWN, k), alarm
            for side in range(2):
                more, more_loss, more_alarms = load(near.at[kind, side, chunk(k)], kind)
                values += more
                if kind == 0:
                    loss += more_loss
                    alarms = jnp.maximum(alarms, more_alarms)
            store(kind, OWN, k, values, loss, alarms)
        for kind in range(2):
            if k == 0:
                back[kind, :groups] = away[kind, OWN, :groups]
            else:
                copy(
                    away.at[kind, OWN, chunk(k)],
                    back.at[kind, chunk(facing(k))],
                    sb.at[kind, k],
                    rb.at[kind, facing(k)],
                    peer(k),
                ).start()

    for kind, out in ((0, out_img), (1, out_txt)):
        for k in range(1, PEERS):
            returned(kind, k).wait_recv()
        steps = back[kind].astype(jnp.int32).reshape(block_rows, width + EXTRA)
        high = lax.shift_right_arithmetic(steps, 8)
        low = steps - lax.shift_left(high, 8)
        pick = layout[:, :block_rows]
        high = dot(pick, high.astype(F32).astype(BF16), 1, 0)
        low = dot(pick, low.astype(F32).astype(BF16), 1, 0)
        grad, loss, _ = decode(high * 256.0 + low, width, kind == 0)
        if kind == 0:
            loss = jnp.broadcast_to(loss * (1.0 / (RING * RING * pairs)), (pairs, pairs))
            out_loss[...] = jnp.transpose(loss)[0:1]
            alarms = jnp.max(steps[:, width:].astype(F32), axis=0, keepdims=True)
            out_alarm[...] = jnp.broadcast_to(alarms, (8, EXTRA))
        along = jnp.sum(unit[kind] * grad, axis=1, keepdims=True)
        out[...] = ((grad - unit[kind] * along) * factor[kind][:, 0:1]).astype(BF16)

    for k in range(PEERS):
        for kind in range(2):
            if k > 0:
                arrived(kind, k).wait_send()
                returned(kind, k).wait_send()
            passed(kind, k).wait_send()
            first(kind, k).wait_send()
            for side in range(2):
                gathered(kind, side, k).wait_send()
                second(kind, side, k).wait_send()


def routed(slots, scale, bias, img_feats, txt_feats, img_head, txt_head, ids, placement):
    pairs, width = img_feats.shape[0], img_head.shape[1]
    deep = img_feats.shape[1]
    wide = width + EXTRA
    block = PEERS * slots // 8
    rows = RING * PEERS * slots
    dma, vmem = pltpu.SemaphoreType.DMA, pl.BlockSpec(memory_space=pltpu.VMEM)
    smem, away = pl.BlockSpec(memory_space=pltpu.SMEM), pl.BlockSpec(memory_space=pl.ANY)
    one, two = dma((2, PEERS)), dma((2, 2, PEERS))
    return pl.pallas_call(
        functools.partial(kernel, slots),
        out_shape=(
            jax.ShapeDtypeStruct((pairs, width), BF16),
            jax.ShapeDtypeStruct((pairs, width), BF16),
            jax.ShapeDtypeStruct((1, pairs), F32),
            jax.ShapeDtypeStruct((8, EXTRA), F32),
        ),
        in_specs=[smem, smem] + [away] * 4 + [vmem] * 2,
        out_specs=(vmem,) * 4,
        scratch_shapes=[
            pltpu.VMEM((2, pairs, deep), BF16),
            pltpu.VMEM((2, deep, width), BF16),
            pltpu.VMEM((pairs, TILE), BF16),
            pltpu.VMEM((2, pairs, width), F32),
            pltpu.VMEM((2, pairs, 128), F32),
            pltpu.VMEM((2, block, 8, width), BF16),
            pltpu.VMEM((2, RING * block, 8, width), BF16),
            pltpu.VMEM((rows, rows), BF16),
            pltpu.VMEM((rows, rows), BF16),
            pltpu.VMEM((rows, 128), F32),
            pltpu.VMEM((2, rows, width), F32),
            pltpu.VMEM((2, RING, block, 8, wide), jnp.int16),
            pltpu.VMEM((2, 2, block, 8, wide), jnp.int16),
            pltpu.VMEM((2, block, 8, wide), jnp.int16),
            pltpu.VMEM((2, block, 8, wide), jnp.int16),
            dma((4,)),
        ]
        + [one] * 2
        + [two] * 2
        + [one] * 4
        + [two] * 2
        + [one] * 2,
        compiler_params=pltpu.CompilerParams(
            collective_id=slots // 8, has_side_effects=True, vmem_limit_bytes=56 * 1024 * 1024
        ),
    )(scale, bias, img_feats, txt_feats, img_head, txt_head, ids, placement)


def final_kernel(img_local, txt_local, img_head, txt_head, loss, out_img, out_txt, out_loss):
    out_img[...] = dot(img_local[...], img_head[...], 1, 1)
    out_txt[...] = dot(txt_local[...], txt_head[...], 1, 1)
    out_loss[...] = loss[...]


def final(img_local, txt_local, img_head, txt_head, loss):
    pairs, width = img_local.shape
    deep = img_head.shape[0]
    parts = 4
    step = deep // parts
    whole = pl.BlockSpec((pairs, width), lambda n: (0, 0))
    some = pl.BlockSpec((step, width), lambda n: (n, 0))
    out = pl.BlockSpec((pairs, step), lambda n: (0, n))
    line = pl.BlockSpec((1, pairs), lambda n: (0, 0))
    return pl.pallas_call(
        final_kernel,
        grid=(parts,),
        out_shape=(
            jax.ShapeDtypeStruct((pairs, deep), F32),
            jax.ShapeDtypeStruct((pairs, deep), F32),
            jax.ShapeDtypeStruct((1, pairs), F32),
        ),
        in_specs=[whole, whole, some, some, line],
        out_specs=(out, out, line),
    )(img_local, txt_local, img_head, txt_head, loss)


FAST = 24


def body(img_feats, txt_feats, img_head, txt_head, cluster_ids, placement, log_scale, bias):
    arguments = (log_scale, bias, img_feats, txt_feats, img_head, txt_head)
    arguments += (cluster_ids.reshape(1, -1), placement.reshape(1, -1))
    img_local, txt_local, loss, alarm = routed(FAST, *arguments)

    def ample():
        img_local, txt_local, loss, _ = routed(MOST, *arguments)
        return final(img_local, txt_local, img_head, txt_head, loss)

    def kept():
        return final(img_local, txt_local, img_head, txt_head, loss)

    img, txt, loss = lax.cond(alarm[0, 4] > 0.5, ample, kept)
    return img, txt, loss.reshape(-1)


def solution(mesh):
    placed = (
        P(("grp", "blk"), None),
        P(("grp", "blk"), None),
        P(),
        P(),
        P(("grp", "blk"), None),
        P(),
        P(),
        P(),
    )
    return jax.shard_map(
        body,
        mesh=mesh,
        in_specs=placed,
        out_specs=(P(("grp", "blk"), None), P(("grp", "blk"), None), P(("grp", "blk"))),
        check_vma=False,
    )
```

time: 99.9 us -> 73.1 us (0.73)
  Pallas kernels: 91.3 us -> 68.4 us
  local copies, waits for them, and re-layouts: 6.35 us -> 1.28 us
    pallas_call x1 -> x2, Pallas kernels: 91.3 us -> 68.4 us  [the longest x1 63.9 us: routed(): pl.pallas_call(functools.partial(kernel, slots), out_shape=(jax.ShapeDtyp...]
    unnamed x3 -> x10, local copies, waits for them, and re-layouts: 5.16 us -> 0.02 us
    slice x0 -> x1, local copies, waits for them, and re-layouts: none -> 1.26 us  [body(): img, txt, loss = lax.cond(alarm[0, 4] > 0.5, ample, kept)]
    squeeze x1 -> x0, local copies, waits for them, and re-layouts: 1.19 us -> none  [body(): return (img, txt, loss[0])]
where the time goes in v2:
time: 73.1 us; the launch traced here: 72.4 us
  Pallas kernels  68.4 us (94%)
  between operations  2.67 us (4%)
  local copies, waits for them, and re-layouts  1.28 us (2%)
    pallas_call x1, Pallas kernels, routed(): pl.pallas_call(functools.partial(kernel, slots), out_shape=(jax.ShapeDtyp...  63.9 us
    pallas_call x1, Pallas kernels, final(): pl.pallas_call(final_kernel, grid=(parts,), out_shape=(jax.ShapeDtypeStru...  4.48 us

profile of v2, /device:TPU:1, one launch (start us, length us, event | category | flops | bytes accessed | tf_op | source)
XLA Modules:
  0.0 72.4 jit_solution(17521666865832168509)
XLA Ops:
  1.9 0.0 copy-start
  1.9 0.0 copy-start.1
  1.9 0.0 copy-start.2
  2.0 0.0 copy-start.3
  2.0 0.0 copy-start.4
  2.0 63.9 %shard_map.105 = (bf16[128,1024]{1,0:T(8,128)(2,1)S(1)}, bf16[128,1024]{1,0:T(8,128)(2,1)S(1)}, f32[1,128]{1,0:T(1,128)S(1)}, f32[8,128]{1,0:T(8,128)}) custom-call(f32[1]{0:T(128)S(6)} %copy.19.scale_ref, f32[1]{0:T(128)S(6)} %copy.20.bias_ref, bf16[128,1024]{1,0:T(8,128)(2,1)} %img_feats.1, bf16[128,1024]{1,0:T(8,128)(2,1)} %txt_feats.1, ...), custom_call_target="tpu_custom_call" | custom-call | tf_op jit(solution)/shard_map/pallas_call | solution.py:475
  65.9 1.3 %slice.3 = f32[1,1]{1,0:T(1,128)} slice(f32[8,128]{1,0:T(8,128)} %get-tuple-element.62), slice={[0:1], [4:5]} | slice | bytes 8 | tf_op jit(solution)/shard_map/slice | solution.py:557
  67.8 0.0 copy-done
  67.8 0.0 copy-done.1
  67.8 0.0 copy-done.2
  67.9 0.0 copy-done.3
  67.9 0.0 copy-done.4
  67.9 4.5 %conditional.1 = (f32[128,1024]{1,0:T(8,128)}, f32[128,1024]{1,0:T(8,128)}, f32[128]{0:T(128)}) conditional(s32[]{:T(128)} %bitcast.4, (bf16[128,1024]{1,0:T(8,128)(2,1)S(1)}, bf16[128,1024]{1,0:T(8,128)(2,1)S(1)}, bf16[1024,1024]{1,0:T(8,128)(2,1)S(1)}, bf16[1024,1024]{1,0:T(8,128)(2,1)}, f32[1,128]{1,0:T(1,128)S(1)}) %tuple.23, (f32[1]{0:T(128)}, ...), branch_computations={%region_0.0_spmd, %region_1.0_spmd} | conditional | bytes 24 | solution.py:557
  67.9 4.5 %branch_0_fun.1 = (f32[128,1024]{1,0:T(8,128)}, f32[128,1024]{1,0:T(8,128)}, f32[1,128]{1,0:T(1,128)}) custom-call(bf16[128,1024]{1,0:T(8,128)(2,1)S(1)} %get-tuple-element.33.img_local, bf16[128,1024]{1,0:T(8,128)(2,1)S(1)} %get-tuple-element.34.txt_local, bf16[1024,1024]{1,0:T(8,128)(2,1)S(1)} %get-tuple-element.35.img_head, ...), custom_call_target="tpu_custom_call" | custom-call | tf_op jit(solution)/shard_map/cond/branch_0_fun/pallas_call | solution.py:529
Async XLA Ops:
  1.9 65.9 %copy-start = (bf16[1024,1024]{1,0:T(8,128)(2,1)S(1)}, bf16[1024,1024]{1,0:T(8,128)(2,1)}, u32[]{:S(2)}) copy-start(bf16[1024,1024]{1,0:T(8,128)(2,1)} %img_head.1) | copy-start | bytes 6291460
  1.9 65.9 %copy-start.1 = (bf16[128,1024]{1,0:T(8,128)(2,1)S(1)}, bf16[128,1024]{1,0:T(8,128)(2,1)}, u32[]{:S(2)}) copy-start(bf16[128,1024]{1,0:T(8,128)(2,1)} %img_feats.1) | copy-start | bytes 786436
  1.9 65.9 %copy-start.2 = (bf16[128,1024]{1,0:T(8,128)(2,1)S(1)}, bf16[128,1024]{1,0:T(8,128)(2,1)}, u32[]{:S(2)}) copy-start(bf16[128,1024]{1,0:T(8,128)(2,1)} %txt_feats.1) | copy-start | bytes 786436
  2.0 65.9 %copy-start.3 = (s32[128,1]{0,1:T(1,128)S(1)}, s32[128,1]{0,1:T(1,128)}, u32[]{:S(2)}) copy-start(s32[128,1]{0,1:T(1,128)} %param.14) | copy-start | bytes 1540
  2.0 65.9 %copy-start.4 = (s32[128]{0:T(128)S(1)}, s32[128]{0:T(128)}, u32[]{:S(2)}) copy-start(s32[128]{0:T(128)} %param.15) | copy-start | bytes 1540

commit v3 on v2

--- a/solution.py
+++ b/solution.py
@@ -59,18 +59,22 @@
 
 def kernel(
     slots,
-    scale_ref,
-    bias_ref,
+    scale_in,
+    bias_in,
     img_feats,
     txt_feats,
     img_head,
     txt_head,
-    ids,
-    placement,
+    ids_in,
+    placement_in,
     out_img,
     out_txt,
     out_loss,
     out_alarm,
+    scale,
+    bias,
+    ids,
+    placement,
     feats,
     head,
     layout,
@@ -91,6 +95,7 @@
     ra,
     sg,
     rg,
+    rh,
     sl,
     rl,
     s1,
@@ -134,16 +139,23 @@
             device_id_type=MESH,
         )
 
+    def done(ref, sem):
+        pltpu.make_async_copy(ref, ref, sem).wait()
+
     def chunk(k, at=0):
         return pl.ds(at * block + k * groups, groups)
 
     loads = []
     for n, (src, dst) in enumerate(
         (
+            (ids_in, ids),
+            (placement_in, placement),
             (img_feats, feats.at[0]),
             (img_head, head.at[0]),
             (txt_feats, feats.at[1]),
             (txt_head, head.at[1]),
+            (scale_in, scale),
+            (bias_in, bias),
         )
     ):
         loads.append(pltpu.make_async_copy(src, dst, si.at[n]))
@@ -158,6 +170,8 @@
                 barrier, inc=1, device_id=neighbour(kind, side), device_id_type=MESH
             )
 
+    loads[0].wait()
+    loads[1].wait()
     lane = lax.broadcasted_iota(jnp.int32, (pairs, 128), 1)
     row = lax.broadcasted_iota(jnp.int32, (pairs, 128), 0)
     lane_f = lane.astype(F32)
@@ -192,7 +206,7 @@
         return copy(
             pack.at[kind, chunk(k)],
             held.at[kind, chunk(k)],
-            sa.at[kind, k],
+            sa.at[kind],
             ra.at[kind, k],
             peer(k),
         )
@@ -201,8 +215,8 @@
         return copy(
             held.at[kind, chunk(k)],
             held.at[kind, chunk(k, PREV if side == 0 else NEXT)],
-            sg.at[kind, side, k],
-            rg.at[kind, side, k],
+            sg.at[kind, side],
+            rg.at[kind, k] if k % 2 == side else rh.at[kind, side],
             neighbour(kind, side),
         )
 
@@ -211,14 +225,23 @@
         return copy(
             held.at[kind, chunk(k, PREV if side == 0 else NEXT)],
             held.at[kind, chunk(k, FAR)],
-            sl.at[kind, k],
-            rl.at[kind, k],
+            sl.at[kind],
+            rl.at[kind],
             neighbour(kind, side),
         )
 
-    for kind in range(2):
-        loads[2 * kind].wait()
-        loads[2 * kind + 1].wait()
+    def send(kind, k):
+        copy(
+            pack.at[kind, chunk(k)],
+            held.at[kind, chunk(facing(k))],
+            sa.at[kind],
+            ra.at[kind, facing(k)],
+            peer(k),
+        ).start()
+
+    for kind in range(2):
+        loads[2 * kind + 2].wait()
+        loads[2 * kind + 3].wait()
         raw = dot(feats[kind], head[kind], 1, 0)
         scale_back = lax.rsqrt(jnp.sum(raw * raw, axis=1, keepdims=True) + EPS)
         unit[kind] = raw * scale_back
@@ -230,35 +253,60 @@
         held[kind, :groups] = pack[kind, :groups]
         if kind == 0:
             pl.semaphore_wait(barrier, PEERS - 1 + 4)
-        for k in range(1, PEERS):
-            copy(
-                pack.at[kind, chunk(k)],
-                held.at[kind, chunk(facing(k))],
-                sa.at[kind, k],
-                ra.at[kind, facing(k)],
-                peer(k),
-            ).start()
+        for k in (1, 2, 4, 3, 5):
+            send(kind, k)
         for side in range(2):
             gathered(kind, side, 0).start()
-
-    def pass_on(k):
-        for kind in range(2):
-            gathered(kind, k % 2, k).wait_recv()
-            passed(kind, k).start()
-
-    for k in range(1, PEERS):
-        for kind in range(2):
-            arrived(kind, k).wait_recv()
-            for side in range(2):
-                gathered(kind, side, k).start()
-        pass_on(k - 1)
-    pass_on(PEERS - 1)
-    for k in range(PEERS):
-        for kind in range(2):
-            gathered(kind, 1 - k % 2, k).wait_recv()
-
-    scale_t = jnp.exp(jnp.full((1, 1), scale_ref[0], F32))
-    shift = bias_ref[0]
+    for kind in range(2):
+        for k in (6, 7):
+            send(kind, k)
+
+    def take(kind, k):
+        arrived(kind, k).wait_recv()
+        for side in range(2):
+            gathered(kind, side, k).start()
+
+    def pass_on(kind, k):
+        gathered(kind, k % 2, k).wait_recv()
+        passed(kind, k).start()
+
+    take(0, 1)
+    take(1, 1)
+    take(0, 2)
+    take(0, 4)
+    pass_on(0, 0)
+    take(0, 3)
+    take(0, 5)
+    pass_on(1, 0)
+    pass_on(0, 1)
+    take(1, 2)
+    take(1, 4)
+    pass_on(1, 1)
+    pass_on(0, 2)
+    take(1, 3)
+    take(1, 5)
+    pass_on(0, 4)
+    pass_on(0, 3)
+    pass_on(0, 5)
+    take(0, 6)
+    take(0, 7)
+    pass_on(1, 2)
+    pass_on(1, 4)
+    take(1, 6)
+    take(1, 7)
+    pass_on(1, 3)
+    pass_on(1, 5)
+    for k in (6, 7):
+        for kind in range(2):
+            pass_on(kind, k)
+    for kind in range(2):
+        for side in range(2):
+            done(held.at[kind, pl.ds(0, block // 2)], rh.at[kind, side])
+
+    loads[6].wait()
+    loads[7].wait()
+    scale_t = jnp.exp(scale[...])
+    shift = bias[...]
     first_lane = jnp.where(lax.broadcasted_iota(jnp.int32, (8, 128), 1) == 0, 1.0, 0.0)
     losses[...] = jnp.zeros_like(losses)
 
@@ -295,9 +343,8 @@
     def _(t):
         tile_of(lax.div(t, early), lax.rem(t, early), False)
 
-    for k in range(PEERS):
-        for kind in range(2):
-            passed(kind, k).wait_recv()
+    for kind in range(2):
+        done(held.at[kind, pl.ds(0, block)], rl.at[kind])
 
     @pl.loop(0, early)
     def _(t):
@@ -348,18 +395,18 @@
     def first(kind, k):
         return copy(
             away.at[kind, FAR, chunk(k)],
-            far.at[kind, chunk(k)],
-            s1.at[kind, k],
-            r1.at[kind, k],
+            far.at[k, kind],
+            s1.at[kind],
+            r1.at[k],
             neighbour(kind, k % 2),
         )
 
     def second(kind, side, k):
         return copy(
             away.at[kind, NEXT if side == 0 else PREV, chunk(k)],
-            near.at[kind, side, chunk(k)],
-            s2.at[kind, side, k],
-            r2.at[kind, side, k],
+            near.at[k, kind, side],
+            s2.at[kind, side],
+            r2.at[k],
             neighbour(kind, side),
         )
 
@@ -367,8 +414,8 @@
         return copy(
             away.at[kind, OWN, chunk(k)],
             back.at[kind, chunk(k)],
-            sb.at[kind, k],
-            rb.at[kind, k],
+            sb.at[kind],
+            rb.at[kind],
             peer(k),
         )
 
@@ -382,40 +429,34 @@
 
     for kind in range(2):
         terms_of(kind, NEXT, 2)
-        for k in order:
-            n = PREV if k % 2 == 0 else NEXT
-            values = part[kind, at(n, k)]
-            store(kind, n, k, values, loss_of(n, k) if kind == 0 else None, alarm)
+
+    def send_on(k):
+        plain, mixed = (PREV, NEXT) if k % 2 == 0 else (NEXT, PREV)
+        for kind in range(2):
+            values = part[kind, at(plain, k)]
+            store(kind, plain, k, values, loss_of(plain, k) if kind == 0 else None, alarm)
+        for kind in range(2):
             second(kind, 1 - k % 2, k).start()
-
-    for kind in range(2):
-        terms_of(kind, OWN, 1)
-
-    for k in order:
-        n = NEXT if k % 2 == 0 else PREV
-        for kind in range(2):
-            first(kind, k).wait_recv()
-        for kind in range(2):
-            values, loss, alarms = load(far.at[kind, chunk(k)], kind)
-            values += part[kind, at(n, k)]
+        done(far.at[k], r1.at[k])
+        for kind in range(2):
+            values, loss, alarms = load(far.at[k, kind], kind)
+            values += part[kind, at(mixed, k)]
             if kind == 0:
-                loss += loss_of(n, k)
+                loss += loss_of(mixed, k)
                 alarms = jnp.maximum(alarms, alarm)
-            store(kind, n, k, values, loss, alarms)
+            store(kind, mixed, k, values, loss, alarms)
         for kind in range(2):
             second(kind, k % 2, k).start()
 
-    for k in order:
-        for kind in range(2):
-            for side in range(2):
-                second(kind, side, k).wait_recv()
+    def send_back(k):
+        done(near.at[k], r2.at[k])
         for kind in range(2):
             values = part[kind, at(OWN, k)]
             loss, alarms = None, None
             if kind == 0:
                 loss, alarms = loss_of(OWN, k), alarm
             for side in range(2):
-                more, more_loss, more_alarms = load(near.at[kind, side, chunk(k)], kind)
+                more, more_loss, more_alarms = load(near.at[k, kind, side], kind)
                 values += more
                 if kind == 0:
                     loss += more_loss
@@ -428,14 +469,24 @@
                 copy(
                     away.at[kind, OWN, chunk(k)],
                     back.at[kind, chunk(facing(k))],
-                    sb.at[kind, k],
-                    rb.at[kind, facing(k)],
+                    sb.at[kind],
+                    rb.at[kind],
                     peer(k),
                 ).start()
 
+    lag = 2
+    for n, k in enumerate(order):
+        send_on(k)
+        if n == lag - 1:
+            for kind in range(2):
+                terms_of(kind, OWN, 1)
+        if n >= lag:
+            send_back(order[n - lag])
+    for k in order[PEERS - lag :]:
+        send_back(k)
+
     for kind, out in ((0, out_img), (1, out_txt)):
-        for k in range(1, PEERS):
-            returned(kind, k).wait_recv()
+        done(back.at[kind, pl.ds(groups, block - groups)], rb.at[kind])
         steps = back[kind].astype(jnp.int32).reshape(block_rows, width + EXTRA)
         high = lax.shift_right_arithmetic(steps, 8)
         low = steps - lax.shift_left(high, 8)
@@ -446,21 +497,18 @@
         if kind == 0:
             loss = jnp.broadcast_to(loss * (1.0 / (RING * RING * pairs)), (pairs, pairs))
             out_loss[...] = jnp.transpose(loss)[0:1]
-            alarms = jnp.max(steps[:, width:].astype(F32), axis=0, keepdims=True)
-            out_alarm[...] = jnp.broadcast_to(alarms, (8, EXTRA))
+            out_alarm[0] = jnp.max(steps[:, width + 4 : width + 5])
         along = jnp.sum(unit[kind] * grad, axis=1, keepdims=True)
         out[...] = ((grad - unit[kind] * along) * factor[kind][:, 0:1]).astype(BF16)
 
-    for k in range(PEERS):
-        for kind in range(2):
-            if k > 0:
-                arrived(kind, k).wait_send()
-                returned(kind, k).wait_send()
-            passed(kind, k).wait_send()
-            first(kind, k).wait_send()
-            for side in range(2):
-                gathered(kind, side, k).wait_send()
-                second(kind, side, k).wait_send()
+    for kind in range(2):
+        done(pack.at[kind, pl.ds(groups, block - groups)], sa.at[kind])
+        done(held.at[kind, pl.ds(0, block)], sl.at[kind])
+        done(away.at[kind, FAR], s1.at[kind])
+        done(away.at[kind, OWN, pl.ds(groups, block - groups)], sb.at[kind])
+        for side in range(2):
+            done(held.at[kind, pl.ds(0, block)], sg.at[kind, side])
+            done(away.at[kind, FAR], s2.at[kind, side])
 
 
 def routed(slots, scale, bias, img_feats, txt_feats, img_head, txt_head, ids, placement):
@@ -471,18 +519,21 @@
     rows = RING * PEERS * slots
     dma, vmem = pltpu.SemaphoreType.DMA, pl.BlockSpec(memory_space=pltpu.VMEM)
     smem, away = pl.BlockSpec(memory_space=pltpu.SMEM), pl.BlockSpec(memory_space=pl.ANY)
-    one, two = dma((2, PEERS)), dma((2, 2, PEERS))
     return pl.pallas_call(
         functools.partial(kernel, slots),
         out_shape=(
             jax.ShapeDtypeStruct((pairs, width), BF16),
             jax.ShapeDtypeStruct((pairs, width), BF16),
             jax.ShapeDtypeStruct((1, pairs), F32),
-            jax.ShapeDtypeStruct((8, EXTRA), F32),
+            jax.ShapeDtypeStruct((1,), jnp.int32),
         ),
-        in_specs=[smem, smem] + [away] * 4 + [vmem] * 2,
-        out_specs=(vmem,) * 4,
+        in_specs=[away] * 8,
+        out_specs=(vmem, vmem, vmem, smem),
         scratch_shapes=[
+            pltpu.VMEM((1, 1), F32),
+            pltpu.VMEM((1, 1), F32),
+            pltpu.VMEM((1, pairs), jnp.int32),
+            pltpu.VMEM((1, pairs), jnp.int32),
             pltpu.VMEM((2, pairs, deep), BF16),
             pltpu.VMEM((2, deep, width), BF16),
             pltpu.VMEM((pairs, TILE), BF16),
@@ -495,47 +546,62 @@
             pltpu.VMEM((rows, 128), F32),
             pltpu.VMEM((2, rows, width), F32),
             pltpu.VMEM((2, RING, block, 8, wide), jnp.int16),
-            pltpu.VMEM((2, 2, block, 8, wide), jnp.int16),
+            pltpu.VMEM((PEERS, 2, 2, slots // 8, 8, wide), jnp.int16),
+            pltpu.VMEM((PEERS, 2, slots // 8, 8, wide), jnp.int16),
             pltpu.VMEM((2, block, 8, wide), jnp.int16),
-            pltpu.VMEM((2, block, 8, wide), jnp.int16),
-            dma((4,)),
-        ]
-        + [one] * 2
-        + [two] * 2
-        + [one] * 4
-        + [two] * 2
-        + [one] * 2,
+            dma((8,)),
+            dma((2,)),
+            dma((2, PEERS)),
+            dma((2, 2)),
+            dma((2, PEERS)),
+            dma((2, 2)),
+            dma((2,)),
+            dma((2,)),
+            dma((2,)),
+            dma((PEERS,)),
+            dma((2, 2)),
+            dma((PEERS,)),
+            dma((2,)),
+            dma((2,)),
+        ],
         compiler_params=pltpu.CompilerParams(
-            collective_id=slots // 8, has_side_effects=True, vmem_limit_bytes=56 * 1024 * 1024
+            collective_id=slots // 8,
+            has_side_effects=True,
+            vmem_limit_bytes=(48 if slots == MOST else 40) * 1024 * 1024,
         ),
     )(scale, bias, img_feats, txt_feats, img_head, txt_head, ids, placement)
 
 
-def final_kernel(img_local, txt_local, img_head, txt_head, loss, out_img, out_txt, out_loss):
-    out_img[...] = dot(img_local[...], img_head[...], 1, 1)
-    out_txt[...] = dot(txt_local[...], txt_head[...], 1, 1)
+def final_kernel(
+    img_local, txt_local, img_head, txt_head, loss, out_img, out_txt, out_loss, done, sems
+):
+    copies = []
+    for kind, (local, head, out) in enumerate(
+        ((img_local, img_head, out_img), (txt_local, txt_head, out_txt))
+    ):
+        done[kind] = dot(local[...], head[...], 1, 1)
+        copies.append(pltpu.make_async_copy(done.at[kind], out, sems.at[kind]))
+        copies[-1].start()
     out_loss[...] = loss[...]
+    for copy in copies:
+        copy.wait()
 
 
 def final(img_local, txt_local, img_head, txt_head, loss):
     pairs, width = img_local.shape
     deep = img_head.shape[0]
-    parts = 4
-    step = deep // parts
-    whole = pl.BlockSpec((pairs, width), lambda n: (0, 0))
-    some = pl.BlockSpec((step, width), lambda n: (n, 0))
-    out = pl.BlockSpec((pairs, step), lambda n: (0, n))
-    line = pl.BlockSpec((1, pairs), lambda n: (0, 0))
+    vmem, away = pl.BlockSpec(memory_space=pltpu.VMEM), pl.BlockSpec(memory_space=pl.ANY)
     return pl.pallas_call(
         final_kernel,
-        grid=(parts,),
         out_shape=(
             jax.ShapeDtypeStruct((pairs, deep), F32),
             jax.ShapeDtypeStruct((pairs, deep), F32),
             jax.ShapeDtypeStruct((1, pairs), F32),
         ),
-        in_specs=[whole, whole, some, some, line],
-        out_specs=(out, out, line),
+        in_specs=[vmem] * 5,
+        out_specs=(away, away, vmem),
+        scratch_shapes=[pltpu.VMEM((2, pairs, deep), F32), pltpu.SemaphoreType.DMA((2,))],
+        compiler_params=pltpu.CompilerParams(vmem_limit_bytes=12 * 1024 * 1024),
     )(img_local, txt_local, img_head, txt_head, loss)
 
 
@@ -543,7 +609,7 @@
 
 
 def body(img_feats, txt_feats, img_head, txt_head, cluster_ids, placement, log_scale, bias):
-    arguments = (log_scale, bias, img_feats, txt_feats, img_head, txt_head)
+    arguments = (log_scale.reshape(1, 1), bias.reshape(1, 1), img_feats, txt_feats, img_head, txt_head)
     arguments += (cluster_ids.reshape(1, -1), placement.reshape(1, -1))
     img_local, txt_local, loss, alarm = routed(FAST, *arguments)
 
@@ -554,7 +620,7 @@
     def kept():
         return final(img_local, txt_local, img_head, txt_head, loss)
 
-    img, txt, loss = lax.cond(alarm[0, 4] > 0.5, ample, kept)
+    img, txt, loss = lax.cond(alarm[0] > 0, ample, kept)
     return img, txt, loss.reshape(-1)
 
 

time: 73.1 us -> 62.1 us (0.85)
  Pallas kernels: 68.4 us -> 59 us
  local copies, waits for them, and re-layouts: 1.28 us -> 0.03 us
    pallas_call x1, Pallas kernels: 63.9 us -> 56.1 us  [routed(): pl.pallas_call(functools.partial(kernel, slots), out_shape=(jax.ShapeDtyp...]
    pallas_call x1, Pallas kernels: 4.48 us -> 2.83 us  [final(): pl.pallas_call(final_kernel, out_shape=(jax.ShapeDtypeStruct((pairs, deep...]
    slice x1 -> x0, local copies, waits for them, and re-layouts: 1.26 us -> none  [body(): img, txt, loss = lax.cond(alarm[0, 4] > 0.5, ample, kept)]
where the time goes in v3:
time: 62.1 us; the launch traced here: 62 us
  Pallas kernels  59 us (95%)
  between operations  2.81 us (5%)
    pallas_call x1, Pallas kernels, routed(): pl.pallas_call(functools.partial(kernel, slots), out_shape=(jax.ShapeDtyp...  56.1 us
    pallas_call x1, Pallas kernels, final(): pl.pallas_call(final_kernel, out_shape=(jax.ShapeDtypeStruct((pairs, deep...  2.83 us

profile of v3, /device:TPU:1, one launch (start us, length us, event | category | flops | bytes accessed | tf_op | source)
XLA Modules:
  0.0 62.0 jit_solution(7875272047498973924)
XLA Ops:
  1.9 0.0 copy-start
  1.9 0.0 copy-start.1
  1.9 0.0 copy-start.2
  2.0 0.0 copy-start.3
  2.0 0.0 copy-start.4
  2.0 0.0 copy-start.5
  2.0 56.1 %shard_map.105 = (bf16[128,1024]{1,0:T(8,128)(2,1)S(1)}, bf16[128,1024]{1,0:T(8,128)(2,1)S(1)}, f32[1,128]{1,0:T(1,128)S(1)}, s32[1]{0:T(128)}) custom-call(f32[1,1]{1,0:T(1,128)} %bitcast.7.scale_in, f32[1,1]{1,0:T(1,128)} %bitcast.8.bias_in, bf16[128,1024]{1,0:T(8,128)(2,1)} %img_feats.1, bf16[128,1024]{1,0:T(8,128)(2,1)} %txt_feats.1, ...), custom_call_target="tpu_custom_call" | custom-call | tf_op jit(solution)/shard_map/pallas_call | solution.py:522
  58.7 0.0 copy-done
  58.8 0.0 copy-done.1
  58.8 0.0 copy-done.2
  58.8 0.0 copy-done.3
  58.8 0.0 copy-done.4
  58.8 0.0 copy-done.5
  58.8 3.0 %conditional.1 = (f32[128,1024]{1,0:T(8,128)}, f32[128,1024]{1,0:T(8,128)}, f32[128]{0:T(128)}) conditional(s32[]{:T(128)} %bitcast.6, (bf16[128,1024]{1,0:T(8,128)(2,1)S(1)}, bf16[128,1024]{1,0:T(8,128)(2,1)S(1)}, bf16[1024,1024]{1,0:T(8,128)(2,1)S(1)}, bf16[1024,1024]{1,0:T(8,128)(2,1)S(1)}, f32[1,128]{1,0:T(1,128)S(1)}) %tuple.25, ...), branch_computations={%region_0.0_spmd, %region_1.0_spmd} | conditional | bytes 24 | solution.py:623
  58.8 2.8 %branch_0_fun.1 = (f32[128,1024]{1,0:T(8,128)}, f32[128,1024]{1,0:T(8,128)}, f32[1,128]{1,0:T(1,128)}) custom-call(bf16[128,1024]{1,0:T(8,128)(2,1)S(1)} %get-tuple-element.33.img_local, bf16[128,1024]{1,0:T(8,128)(2,1)S(1)} %get-tuple-element.34.txt_local, bf16[1024,1024]{1,0:T(8,128)(2,1)S(1)} %get-tuple-element.35.img_head, ...), custom_call_target="tpu_custom_call" | custom-call | tf_op jit(solution)/shard_map/cond/branch_0_fun/pallas_call | solution.py:594
Async XLA Ops:
  1.9 56.8 %copy-start = (bf16[1024,1024]{1,0:T(8,128)(2,1)S(1)}, bf16[1024,1024]{1,0:T(8,128)(2,1)}, u32[]{:S(2)}) copy-start(bf16[1024,1024]{1,0:T(8,128)(2,1)} %img_head.1) | copy-start | bytes 6291460
  1.9 56.8 %copy-start.1 = (bf16[1024,1024]{1,0:T(8,128)(2,1)S(1)}, bf16[1024,1024]{1,0:T(8,128)(2,1)}, u32[]{:S(2)}) copy-start(bf16[1024,1024]{1,0:T(8,128)(2,1)} %txt_head.1) | copy-start | bytes 6291460
  1.9 56.8 %copy-start.2 = (bf16[128,1024]{1,0:T(8,128)(2,1)S(1)}, bf16[128,1024]{1,0:T(8,128)(2,1)}, u32[]{:S(2)}) copy-start(bf16[128,1024]{1,0:T(8,128)(2,1)} %img_feats.1) | copy-start | bytes 786436
  2.0 56.8 %copy-start.3 = (bf16[128,1024]{1,0:T(8,128)(2,1)S(1)}, bf16[128,1024]{1,0:T(8,128)(2,1)}, u32[]{:S(2)}) copy-start(bf16[128,1024]{1,0:T(8,128)(2,1)} %txt_feats.1) | copy-start | bytes 786436
  2.0 56.8 %copy-start.4 = (s32[128,1]{0,1:T(1,128)S(1)}, s32[128,1]{0,1:T(1,128)}, u32[]{:S(2)}) copy-start(s32[128,1]{0,1:T(1,128)} %param.14) | copy-start | bytes 1540
  2.0 56.8 %copy-start.5 = (s32[128]{0:T(128)S(1)}, s32[128]{0:T(128)}, u32[]{:S(2)}) copy-start(s32[128]{0:T(128)} %param.15) | copy-start | bytes 1540

commit v4 on v3

--- a/solution.py
+++ b/solution.py
@@ -16,6 +16,9 @@
 EXTRA = 128
 LEVELS = 32000.0
 AROUND = (0, 1, 3, 2)
+ARRIVALS = (1, 2, 4, 3, 5, 6, 7)
+SOON = 3
+LAG = 6
 FACING = (0, 2, 1, 3)
 OWN, NEXT, PREV, FAR = range(4)
 MESH = pl.DeviceIdType.MESH
@@ -28,9 +31,8 @@
     return lax.dot_general(a, b, (((da,), (db,)), ((), ())), preferred_element_type=F32)
 
 
-def encode(values, loss, alarm):
+def encode(values, top, loss, alarm):
     rows = values.shape[0]
-    top = jnp.max(jnp.abs(values), axis=1, keepdims=True)
     grade = jnp.ceil(8.0 * jnp.log2(jnp.maximum(top, 1e-30)))
     steps = jnp.round(values * (LEVELS * jnp.exp2(-0.125 * grade)))
     lane = lax.broadcasted_iota(jnp.int32, (rows, EXTRA), 1)
@@ -49,12 +51,13 @@
 
 def decode(coded, width, with_loss):
     extra = coded[:, width:]
-    values = coded[:, :width] * (jnp.exp2(0.125 * extra[:, 0:1]) * (1.0 / LEVELS))
+    top = jnp.exp2(0.125 * extra[:, 0:1])
+    values = coded[:, :width] * (top * (1.0 / LEVELS))
     if not with_loss:
-        return values, None, None
+        return values, top, None, None
     scale = jnp.exp2(0.125 * extra[:, 1:2]) * (1.0 / LEVELS)
     loss = (extra[:, 2:3] + extra[:, 3:4] * (1.0 / LEVELS)) * scale
-    return values, loss, extra[:, 4:5]
+    return values, top, loss, extra[:, 4:5]
 
 
 def kernel(
@@ -86,6 +89,7 @@
     turned,
     losses,
     part,
+    tops,
     away,
     near,
     far,
@@ -253,12 +257,12 @@
         held[kind, :groups] = pack[kind, :groups]
         if kind == 0:
             pl.semaphore_wait(barrier, PEERS - 1 + 4)
-        for k in (1, 2, 4, 3, 5):
+        for k in ARRIVALS[:SOON]:
             send(kind, k)
         for side in range(2):
             gathered(kind, side, 0).start()
-    for kind in range(2):
-        for k in (6, 7):
+    for k in ARRIVALS[SOON:]:
+        for kind in range(2):
             send(kind, k)
 
     def take(kind, k):
@@ -270,35 +274,15 @@
         gathered(kind, k % 2, k).wait_recv()
         passed(kind, k).start()
 
-    take(0, 1)
-    take(1, 1)
-    take(0, 2)
-    take(0, 4)
-    pass_on(0, 0)
-    take(0, 3)
-    take(0, 5)
-    pass_on(1, 0)
-    pass_on(0, 1)
-    take(1, 2)
-    take(1, 4)
-    pass_on(1, 1)
-    pass_on(0, 2)
-    take(1, 3)
-    take(1, 5)
-    pass_on(0, 4)
-    pass_on(0, 3)
-    pass_on(0, 5)
-    take(0, 6)
-    take(0, 7)
-    pass_on(1, 2)
-    pass_on(1, 4)
-    take(1, 6)
-    take(1, 7)
-    pass_on(1, 3)
-    pass_on(1, 5)
-    for k in (6, 7):
-        for kind in range(2):
-            pass_on(kind, k)
+    takes = [(kind, k) for k in ARRIVALS for kind in range(2)]
+    passes = [(kind, k) for k in (0,) + ARRIVALS for kind in range(2)]
+    for n, one in enumerate(takes):
+        take(*one)
+        if n >= LAG:
+            pass_on(*passes[n - LAG])
+    for one in passes[len(takes) - LAG :]:
+        pass_on(*one)
+
     for kind in range(2):
         for side in range(2):
             done(held.at[kind, pl.ds(0, block // 2)], rh.at[kind, side])
@@ -328,8 +312,8 @@
         whole = 1.0 + odds
         inverse = 1.0 / whole
         terms = jnp.log(whole) + (odds - (whole - 1.0)) * inverse
-        rows = pl.ds(pl.multiple_of(i * TILE, TILE), TILE)
-        columns = pl.ds(pl.multiple_of(j * TILE, TILE), TILE)
+        rows = pl.ds(i * TILE, TILE)
+        columns = pl.ds(j * TILE, TILE)
         losses[rows] += terms[:, :128] + terms[:, 128:]
         weights = odds * inverse * jnp.where(images[:, 0:1].astype(F32) < 1.5, scale_t, 0.0)
         if with_own:
@@ -339,19 +323,15 @@
 
     tile_of(0, 0, True)
 
-    @pl.loop(1, early * early)
-    def _(t):
-        tile_of(lax.div(t, early), lax.rem(t, early), False)
+    for t in range(1, early * early):
+        tile_of(t // early, t % early, False)
 
     for kind in range(2):
         done(held.at[kind, pl.ds(0, block)], rl.at[kind])
 
-    @pl.loop(0, early)
-    def _(t):
+    for t in range(early):
         tile_of(t, early, False)
-
-    @pl.loop(0, early + 1)
-    def _(t):
+    for t in range(early + 1):
         tile_of(early, t, False)
 
     alarm = None
@@ -368,21 +348,34 @@
     def terms_of(kind, start, size):
         weights = coef if kind == 0 else turned
 
-        @pl.loop(0, width // TILE)
-        def _(q):
-            lanes = pl.ds(pl.multiple_of(q * TILE, TILE), TILE)
+        for q in range(width // TILE):
+            lanes = pl.ds(q * TILE, TILE)
             others = held[1 - kind, :, :, lanes].reshape(RING * block_rows, TILE)
             rows = pl.ds(start * block_rows, size * block_rows)
             part[kind, rows, lanes] = dot(weights[rows], others, 1, 0)
 
+        rows = pl.ds(start * block_rows, size * block_rows)
+        top = jnp.max(jnp.abs(part[kind, rows]), axis=1, keepdims=True)
+        tops[kind, rows] = jnp.broadcast_to(top, (size * block_rows, 128))
+
     def at(n, k):
         return pl.ds(n * block_rows + k * slots, slots)
 
-    def loss_of(n, k):
-        return jnp.sum(losses[at(n, k)], axis=1, keepdims=True)
-
-    def store(kind, n, k, values, loss, alarm):
-        steps, extra = encode(values, loss, alarm)
+    total = jnp.sum(losses[...], axis=1, keepdims=True)
+    losses[...] = jnp.broadcast_to(total, losses.shape)
+
+    def mine(kind, n, k):
+        rows = at(n, k)
+        loss = losses[rows][:, 0:1] if kind == 0 else None
+        alarms = alarm if kind == 0 else None
+        return part[kind, rows], tops[kind, rows][:, 0:1], loss, alarms
+
+    def both(one, other):
+        sums = [a if b is None else a + b for a, b in zip(one[:3], other[:3])]
+        return (*sums, None if one[3] is None else jnp.maximum(one[3], other[3]))
+
+    def store(kind, n, k, terms):
+        steps, extra = encode(*terms)
         steps = steps.reshape(groups, 8, width).astype(jnp.int32)
         away[kind, n, chunk(k), :, :width] = steps.astype(jnp.int16)
         extra = extra.reshape(groups, 8, EXTRA).astype(jnp.int32)
@@ -419,49 +412,47 @@
             peer(k),
         )
 
-    order = tuple(range(PEERS - 1, -1, -1))
+    def plain(k):
+        return PREV if k % 2 == 0 else NEXT
+
+    def mixed(k):
+        return NEXT if k % 2 == 0 else PREV
+
+    couples = ((7, 6), (5, 2), (4, 3), (1, 0))
+    order = tuple(k for couple in couples for k in couple)
     for kind in range(2):
         terms_of(kind, FAR, 1)
-        for k in order:
-            values = part[kind, at(FAR, k)]
-            store(kind, FAR, k, values, loss_of(FAR, k) if kind == 0 else None, alarm)
-            first(kind, k).start()
+        for some in (order[:2], order[2:]):
+            for k in some:
+                store(kind, FAR, k, mine(kind, FAR, k))
+            for k in some[:4]:
+                first(kind, k).start()
 
     for kind in range(2):
         terms_of(kind, NEXT, 2)
-
-    def send_on(k):
-        plain, mixed = (PREV, NEXT) if k % 2 == 0 else (NEXT, PREV)
-        for kind in range(2):
-            values = part[kind, at(plain, k)]
-            store(kind, plain, k, values, loss_of(plain, k) if kind == 0 else None, alarm)
-        for kind in range(2):
+        for k in order:
+            store(kind, plain(k), k, mine(kind, plain(k), k))
+        for k in order[:2]:
             second(kind, 1 - k % 2, k).start()
-        done(far.at[k], r1.at[k])
-        for kind in range(2):
-            values, loss, alarms = load(far.at[k, kind], kind)
-            values += part[kind, at(mixed, k)]
-            if kind == 0:
-                loss += loss_of(mixed, k)
-                alarms = jnp.maximum(alarms, alarm)
-            store(kind, mixed, k, values, loss, alarms)
-        for kind in range(2):
-            second(kind, k % 2, k).start()
+
+    def send_on(couple):
+        for k in couple:
+            done(far.at[k], r1.at[k])
+        for k in couple:
+            for kind in range(2):
+                more = load(far.at[k, kind], kind)
+                store(kind, mixed(k), k, both(mine(kind, mixed(k), k), more))
+        for k in couple:
+            for kind in range(2):
+                second(kind, k % 2, k).start()
 
     def send_back(k):
         done(near.at[k], r2.at[k])
         for kind in range(2):
-            values = part[kind, at(OWN, k)]
-            loss, alarms = None, None
-            if kind == 0:
-                loss, alarms = loss_of(OWN, k), alarm
+            terms = mine(kind, OWN, k)
             for side in range(2):
-                more, more_loss, more_alarms = load(near.at[k, kind, side], kind)
-                values += more
-                if kind == 0:
-                    loss += more_loss
-                    alarms = jnp.maximum(alarms, more_alarms)
-            store(kind, OWN, k, values, loss, alarms)
+                terms = both(terms, load(near.at[k, kind, side], kind))
+            store(kind, OWN, k, terms)
         for kind in range(2):
             if k == 0:
                 back[kind, :groups] = away[kind, OWN, :groups]
@@ -474,15 +465,23 @@
                     peer(k),
                 ).start()
 
-    lag = 2
-    for n, k in enumerate(order):
-        send_on(k)
-        if n == lag - 1:
+    for n, couple in enumerate(couples):
+        send_on(couple)
+        if n == 0:
+            for kind in range(2):
+                for k in order[6:]:
+                    first(kind, k).start()
+        if n + 1 < len(couples):
+            for kind in range(2):
+                for k in couples[n + 1]:
+                    second(kind, 1 - k % 2, k).start()
+        if n == 0:
             for kind in range(2):
                 terms_of(kind, OWN, 1)
-        if n >= lag:
-            send_back(order[n - lag])
-    for k in order[PEERS - lag :]:
+        else:
+            for k in couples[n - 1]:
+                send_back(k)
+    for k in couples[-1]:
         send_back(k)
 
     for kind, out in ((0, out_img), (1, out_txt)):
@@ -493,7 +492,7 @@
         pick = layout[:, :block_rows]
         high = dot(pick, high.astype(F32).astype(BF16), 1, 0)
         low = dot(pick, low.astype(F32).astype(BF16), 1, 0)
-        grad, loss, _ = decode(high * 256.0 + low, width, kind == 0)
+        grad, _, loss, _ = decode(high * 256.0 + low, width, kind == 0)
         if kind == 0:
             loss = jnp.broadcast_to(loss * (1.0 / (RING * RING * pairs)), (pairs, pairs))
             out_loss[...] = jnp.transpose(loss)[0:1]
@@ -545,6 +544,7 @@
             pltpu.VMEM((rows, rows), BF16),
             pltpu.VMEM((rows, 128), F32),
             pltpu.VMEM((2, rows, width), F32),
+            pltpu.VMEM((2, rows, 128), F32),
             pltpu.VMEM((2, RING, block, 8, wide), jnp.int16),
             pltpu.VMEM((PEERS, 2, 2, slots // 8, 8, wide), jnp.int16),
             pltpu.VMEM((PEERS, 2, slots // 8, 8, wide), jnp.int16),

time: 62.1 us -> 55.7 us (0.90)
  Pallas kernels: 59 us -> 52.5 us
    pallas_call x1, Pallas kernels: 56.1 us -> 49.6 us  [routed(): pl.pallas_call(functools.partial(kernel, slots), out_shape=(jax.ShapeDtyp...]
where the time goes in v4:
time: 55.7 us; the launch traced here: 55.5 us
  Pallas kernels  52.5 us (94%)
  between operations  2.83 us (5%)
    pallas_call x1, Pallas kernels, routed(): pl.pallas_call(functools.partial(kernel, slots), out_shape=(jax.ShapeDtyp...  49.6 us
    pallas_call x1, Pallas kernels, final(): pl.pallas_call(final_kernel, out_shape=(jax.ShapeDtypeStruct((pairs, deep...  2.82 us

profile of v4, /device:TPU:1, one launch (start us, length us, event | category | flops | bytes accessed | tf_op | source)
XLA Modules:
  0.0 55.5 jit_solution(12348473671835713512)
XLA Ops:
  1.9 0.0 copy-start
  1.9 0.0 copy-start.1
  1.9 0.0 copy-start.2
  2.0 0.0 copy-start.3
  2.0 0.0 copy-start.4
  2.0 0.0 copy-start.5
  2.0 49.6 %shard_map.105 = (bf16[128,1024]{1,0:T(8,128)(2,1)S(1)}, bf16[128,1024]{1,0:T(8,128)(2,1)S(1)}, f32[1,128]{1,0:T(1,128)S(1)}, s32[1]{0:T(128)}) custom-call(f32[1,1]{1,0:T(1,128)} %bitcast.7.scale_in, f32[1,1]{1,0:T(1,128)} %bitcast.8.bias_in, bf16[128,1024]{1,0:T(8,128)(2,1)} %img_feats.1, bf16[128,1024]{1,0:T(8,128)(2,1)} %txt_feats.1, ...), custom_call_target="tpu_custom_call" | custom-call | tf_op jit(solution)/shard_map/pallas_call | solution.py:521
  52.2 0.0 copy-done
  52.3 0.0 copy-done.1
  52.3 0.0 copy-done.2
  52.3 0.0 copy-done.3
  52.3 0.0 copy-done.4
  52.3 0.0 copy-done.5
  52.3 3.1 %conditional.1 = (f32[128,1024]{1,0:T(8,128)}, f32[128,1024]{1,0:T(8,128)}, f32[128]{0:T(128)}) conditional(s32[]{:T(128)} %bitcast.6, (bf16[128,1024]{1,0:T(8,128)(2,1)S(1)}, bf16[128,1024]{1,0:T(8,128)(2,1)S(1)}, bf16[1024,1024]{1,0:T(8,128)(2,1)S(1)}, bf16[1024,1024]{1,0:T(8,128)(2,1)S(1)}, f32[1,128]{1,0:T(1,128)S(1)}) %tuple.25, ...), branch_computations={%region_0.0_spmd, %region_1.0_spmd} | conditional | bytes 24 | solution.py:623
  52.3 2.8 %branch_0_fun.1 = (f32[128,1024]{1,0:T(8,128)}, f32[128,1024]{1,0:T(8,128)}, f32[1,128]{1,0:T(1,128)}) custom-call(bf16[128,1024]{1,0:T(8,128)(2,1)S(1)} %get-tuple-element.33.img_local, bf16[128,1024]{1,0:T(8,128)(2,1)S(1)} %get-tuple-element.34.txt_local, bf16[1024,1024]{1,0:T(8,128)(2,1)S(1)} %get-tuple-element.35.img_head, ...), custom_call_target="tpu_custom_call" | custom-call | tf_op jit(solution)/shard_map/cond/branch_0_fun/pallas_call | solution.py:594
Async XLA Ops:
  1.9 50.3 %copy-start = (bf16[1024,1024]{1,0:T(8,128)(2,1)S(1)}, bf16[1024,1024]{1,0:T(8,128)(2,1)}, u32[]{:S(2)}) copy-start(bf16[1024,1024]{1,0:T(8,128)(2,1)} %img_head.1) | copy-start | bytes 6291460
  1.9 50.3 %copy-start.1 = (bf16[1024,1024]{1,0:T(8,128)(2,1)S(1)}, bf16[1024,1024]{1,0:T(8,128)(2,1)}, u32[]{:S(2)}) copy-start(bf16[1024,1024]{1,0:T(8,128)(2,1)} %txt_head.1) | copy-start | bytes 6291460
  1.9 50.3 %copy-start.2 = (bf16[128,1024]{1,0:T(8,128)(2,1)S(1)}, bf16[128,1024]{1,0:T(8,128)(2,1)}, u32[]{:S(2)}) copy-start(bf16[128,1024]{1,0:T(8,128)(2,1)} %img_feats.1) | copy-start | bytes 786436
  2.0 50.3 %copy-start.3 = (bf16[128,1024]{1,0:T(8,128)(2,1)S(1)}, bf16[128,1024]{1,0:T(8,128)(2,1)}, u32[]{:S(2)}) copy-start(bf16[128,1024]{1,0:T(8,128)(2,1)} %txt_feats.1) | copy-start | bytes 786436
  2.0 50.3 %copy-start.4 = (s32[128,1]{0,1:T(1,128)S(1)}, s32[128,1]{0,1:T(1,128)}, u32[]{:S(2)}) copy-start(s32[128,1]{0,1:T(1,128)} %param.14) | copy-start | bytes 1540
  2.0 50.3 %copy-start.5 = (s32[128]{0:T(128)S(1)}, s32[128]{0:T(128)}, u32[]{:S(2)}) copy-start(s32[128]{0:T(128)} %param.15) | copy-start | bytes 1540

commit v5 on v4

--- a/solution.py
+++ b/solution.py
@@ -32,32 +32,27 @@
 
 
 def encode(values, top, loss, alarm):
-    rows = values.shape[0]
     grade = jnp.ceil(8.0 * jnp.log2(jnp.maximum(top, 1e-30)))
-    steps = jnp.round(values * (LEVELS * jnp.exp2(-0.125 * grade)))
-    lane = lax.broadcasted_iota(jnp.int32, (rows, EXTRA), 1)
-    extra = jnp.where(lane == 0, grade, 0.0)
+    scale = LEVELS * jnp.exp2(-0.125 * grade)
+    steps = [jnp.round(values[:, n : n + EXTRA] * scale) for n in range(0, values.shape[1], EXTRA)]
+    fields = [grade]
     if loss is not None:
         loss_grade = jnp.ceil(8.0 * jnp.log2(jnp.maximum(loss, 1e-30)))
         scaled = loss * (LEVELS * jnp.exp2(-0.125 * loss_grade))
         high = jnp.round(scaled)
         low = jnp.round((scaled - high) * LEVELS)
-        extra = jnp.where(lane == 1, loss_grade, extra)
-        extra = jnp.where(lane == 2, high, extra)
-        extra = jnp.where(lane == 3, low, extra)
-        extra = jnp.where(lane == 4, alarm, extra)
+        fields += [loss_grade, high, low, alarm]
+    lane = lax.broadcasted_iota(jnp.int32, (8, EXTRA), 1)
+    extra = jnp.zeros((8, EXTRA), F32)
+    for r in range(values.shape[0] // 8):
+        for f, field in enumerate(fields):
+            extra = jnp.where(lane == 8 * r + f, field[8 * r : 8 * r + 8], extra)
     return steps, extra
 
 
-def decode(coded, width, with_loss):
-    extra = coded[:, width:]
-    top = jnp.exp2(0.125 * extra[:, 0:1])
-    values = coded[:, :width] * (top * (1.0 / LEVELS))
-    if not with_loss:
-        return values, top, None, None
-    scale = jnp.exp2(0.125 * extra[:, 1:2]) * (1.0 / LEVELS)
-    loss = (extra[:, 2:3] + extra[:, 3:4] * (1.0 / LEVELS)) * scale
-    return values, top, loss, extra[:, 4:5]
+def loss_from(loss_grade, high, low):
+    scale = jnp.exp2(0.125 * loss_grade) * (1.0 / LEVELS)
+    return (high + low * (1.0 / LEVELS)) * scale
 
 
 def kernel(
@@ -366,28 +361,45 @@
 
     def mine(kind, n, k):
         rows = at(n, k)
-        loss = losses[rows][:, 0:1] if kind == 0 else None
-        alarms = alarm if kind == 0 else None
-        return part[kind, rows], tops[kind, rows][:, 0:1], loss, alarms
+        values, top = part[kind, rows], tops[kind, rows]
+        if kind == 1:
+            return values, top, None, None
+        return values, top, losses[rows], jnp.broadcast_to(alarm, (slots, EXTRA))
 
     def both(one, other):
         sums = [a if b is None else a + b for a, b in zip(one[:3], other[:3])]
         return (*sums, None if one[3] is None else jnp.maximum(one[3], other[3]))
 
+    parts = width // EXTRA * groups
+
     def store(kind, n, k, terms):
         steps, extra = encode(*terms)
-        steps = steps.reshape(groups, 8, width).astype(jnp.int32)
-        away[kind, n, chunk(k), :, :width] = steps.astype(jnp.int16)
-        extra = extra.reshape(groups, 8, EXTRA).astype(jnp.int32)
-        away[kind, n, chunk(k), :, width:] = extra.astype(jnp.int16)
+        for l, step in enumerate(steps):
+            step = step.reshape(groups, 8, EXTRA).astype(jnp.int32)
+            away[kind, n, k, l * groups : (l + 1) * groups] = step.astype(jnp.int16)
+        away[kind, n, k, parts] = extra.astype(jnp.int32).astype(jnp.int16)
 
     def load(ref, kind):
-        value = ref[...].astype(F32).reshape(slots, width + EXTRA)
-        return decode(value, width, kind == 0)
+        coded = ref[...].astype(F32)
+        extra = coded[parts]
+
+        def field(f):
+            each = [extra[:, 8 * r + f : 8 * r + f + 1] for r in range(groups)]
+            return jnp.concatenate([jnp.broadcast_to(e, (8, EXTRA)) for e in each], axis=0)
+
+        top = jnp.exp2(0.125 * field(0))
+        step = top * (1.0 / LEVELS)
+        values = [
+            coded[l : l + groups].reshape(slots, EXTRA) * step for l in range(0, parts, groups)
+        ]
+        values = jnp.concatenate(values, axis=1)
+        if kind == 1:
+            return values, top, None, None
+        return values, top, loss_from(field(1), field(2), field(3)), field(4)
 
     def first(kind, k):
         return copy(
-            away.at[kind, FAR, chunk(k)],
+            away.at[kind, FAR, k],
             far.at[k, kind],
             s1.at[kind],
             r1.at[k],
@@ -396,7 +408,7 @@
 
     def second(kind, side, k):
         return copy(
-            away.at[kind, NEXT if side == 0 else PREV, chunk(k)],
+            away.at[kind, NEXT if side == 0 else PREV, k],
             near.at[k, kind, side],
             s2.at[kind, side],
             r2.at[k],
@@ -405,8 +417,8 @@
 
     def returned(kind, k):
         return copy(
-            away.at[kind, OWN, chunk(k)],
-            back.at[kind, chunk(k)],
+            away.at[kind, OWN, k],
+            back.at[kind, k],
             sb.at[kind],
             rb.at[kind],
             peer(k),
@@ -418,7 +430,7 @@
     def mixed(k):
         return NEXT if k % 2 == 0 else PREV
 
-    couples = ((7, 6), (5, 2), (4, 3), (1, 0))
+    couples = ((7, 6), (5, 4), (3, 2), (1, 0))
     order = tuple(k for couple in couples for k in couple)
     for kind in range(2):
         terms_of(kind, FAR, 1)
@@ -455,11 +467,11 @@
             store(kind, OWN, k, terms)
         for kind in range(2):
             if k == 0:
-                back[kind, :groups] = away[kind, OWN, :groups]
+                back[kind, 0] = away[kind, OWN, 0]
             else:
                 copy(
-                    away.at[kind, OWN, chunk(k)],
-                    back.at[kind, chunk(facing(k))],
+                    away.at[kind, OWN, k],
+                    back.at[kind, facing(k)],
                     sb.at[kind],
                     rb.at[kind],
                     peer(k),
@@ -485,15 +497,26 @@
         send_back(k)
 
     for kind, out in ((0, out_img), (1, out_txt)):
-        done(back.at[kind, pl.ds(groups, block - groups)], rb.at[kind])
-        steps = back[kind].astype(jnp.int32).reshape(block_rows, width + EXTRA)
+        done(back.at[kind, pl.ds(1, PEERS - 1)], rb.at[kind])
+        coded = back[kind].astype(jnp.int32)
+        extra = coded[:, parts].reshape(PEERS * 8, EXTRA)
+        extras = [extra] + [pltpu.roll(extra, EXTRA - 8 * r, 1) for r in range(1, groups)]
+        extras = [e.reshape(PEERS, 1, 8, EXTRA) for e in extras]
+        lanes = [
+            coded[:, l : l + groups].reshape(block_rows, EXTRA) for l in range(0, parts, groups)
+        ]
+        lanes.append(jnp.concatenate(extras, axis=1).reshape(block_rows, EXTRA))
+        steps = jnp.concatenate(lanes, axis=1)
         high = lax.shift_right_arithmetic(steps, 8)
         low = steps - lax.shift_left(high, 8)
         pick = layout[:, :block_rows]
         high = dot(pick, high.astype(F32).astype(BF16), 1, 0)
         low = dot(pick, low.astype(F32).astype(BF16), 1, 0)
-        grad, _, loss, _ = decode(high * 256.0 + low, width, kind == 0)
+        own = high * 256.0 + low
+        fields = [own[:, width + f : width + f + 1] for f in range(4)]
+        grad = own[:, :width] * (jnp.exp2(0.125 * fields[0]) * (1.0 / LEVELS))
         if kind == 0:
+            loss = loss_from(*fields[1:])
             loss = jnp.broadcast_to(loss * (1.0 / (RING * RING * pairs)), (pairs, pairs))
             out_loss[...] = jnp.transpose(loss)[0:1]
             out_alarm[0] = jnp.max(steps[:, width + 4 : width + 5])
@@ -504,7 +527,7 @@
         done(pack.at[kind, pl.ds(groups, block - groups)], sa.at[kind])
         done(held.at[kind, pl.ds(0, block)], sl.at[kind])
         done(away.at[kind, FAR], s1.at[kind])
-        done(away.at[kind, OWN, pl.ds(groups, block - groups)], sb.at[kind])
+        done(away.at[kind, OWN, pl.ds(1, PEERS - 1)], sb.at[kind])
         for side in range(2):
             done(held.at[kind, pl.ds(0, block)], sg.at[kind, side])
             done(away.at[kind, FAR], s2.at[kind, side])
@@ -513,7 +536,7 @@
 def routed(slots, scale, bias, img_feats, txt_feats, img_head, txt_head, ids, placement):
     pairs, width = img_feats.shape[0], img_head.shape[1]
     deep = img_feats.shape[1]
-    wide = width + EXTRA
+    parts = width // EXTRA * (slots // 8) + 1
     block = PEERS * slots // 8
     rows = RING * PEERS * slots
     dma, vmem = pltpu.SemaphoreType.DMA, pl.BlockSpec(memory_space=pltpu.VMEM)
@@ -545,10 +568,10 @@
             pltpu.VMEM((rows, 128), F32),
             pltpu.VMEM((2, rows, width), F32),
             pltpu.VMEM((2, rows, 128), F32),
-            pltpu.VMEM((2, RING, block, 8, wide), jnp.int16),
-            pltpu.VMEM((PEERS, 2, 2, slots // 8, 8, wide), jnp.int16),
-            pltpu.VMEM((PEERS, 2, slots // 8, 8, wide), jnp.int16),
-            pltpu.VMEM((2, block, 8, wide), jnp.int16),
+            pltpu.VMEM((2, RING, PEERS, parts, 8, EXTRA), jnp.int16),
+            pltpu.VMEM((PEERS, 2, 2, parts, 8, EXTRA), jnp.int16),
+            pltpu.VMEM((PEERS, 2, parts, 8, EXTRA), jnp.int16),
+            pltpu.VMEM((2, PEERS, parts, 8, EXTRA), jnp.int16),
             dma((8,)),
             dma((2,)),
             dma((2, PEERS)),

time: 55.7 us -> 53.7 us (0.964)
  Pallas kernels: 52.5 us -> 50.4 us
    pallas_call x1, Pallas kernels: 49.6 us -> 47.6 us  [routed(): pl.pallas_call(functools.partial(kernel, slots), out_shape=(jax.ShapeDtyp...]
where the time goes in v5:
time: 53.7 us; the launch traced here: 53.5 us
  Pallas kernels  50.4 us (94%)
  between operations  2.83 us (5%)
    pallas_call x1, Pallas kernels, routed(): pl.pallas_call(functools.partial(kernel, slots), out_shape=(jax.ShapeDtyp...  47.6 us
    pallas_call x1, Pallas kernels, final(): pl.pallas_call(final_kernel, out_shape=(jax.ShapeDtypeStruct((pairs, deep...  2.82 us

profile of v5, /device:TPU:1, one launch (start us, length us, event | category | flops | bytes accessed | tf_op | source)
XLA Modules:
  0.0 53.5 jit_solution(3782065909446680842)
XLA Ops:
  1.9 0.0 copy-start
  1.9 0.0 copy-start.1
  1.9 0.0 copy-start.2
  2.0 0.0 copy-start.3
  2.0 0.0 copy-start.4
  2.0 0.0 copy-start.5
  2.0 47.6 %shard_map.105 = (bf16[128,1024]{1,0:T(8,128)(2,1)S(1)}, bf16[128,1024]{1,0:T(8,128)(2,1)S(1)}, f32[1,128]{1,0:T(1,128)S(1)}, s32[1]{0:T(128)}) custom-call(f32[1,1]{1,0:T(1,128)} %bitcast.7.scale_in, f32[1,1]{1,0:T(1,128)} %bitcast.8.bias_in, bf16[128,1024]{1,0:T(8,128)(2,1)} %img_feats.1, bf16[128,1024]{1,0:T(8,128)(2,1)} %txt_feats.1, ...), custom_call_target="tpu_custom_call" | custom-call | tf_op jit(solution)/shard_map/pallas_call | solution.py:544
  50.2 0.0 copy-done
  50.2 0.0 copy-done.1
  50.2 0.0 copy-done.2
  50.2 0.0 copy-done.3
  50.2 0.0 copy-done.4
  50.2 0.0 copy-done.5
  50.2 3.1 %conditional.1 = (f32[128,1024]{1,0:T(8,128)}, f32[128,1024]{1,0:T(8,128)}, f32[128]{0:T(128)}) conditional(s32[]{:T(128)} %bitcast.6, (bf16[128,1024]{1,0:T(8,128)(2,1)S(1)}, bf16[128,1024]{1,0:T(8,128)(2,1)S(1)}, bf16[1024,1024]{1,0:T(8,128)(2,1)S(1)}, bf16[1024,1024]{1,0:T(8,128)(2,1)S(1)}, f32[1,128]{1,0:T(1,128)S(1)}) %tuple.25, ...), branch_computations={%region_0.0_spmd, %region_1.0_spmd} | conditional | bytes 24 | solution.py:646
  50.3 2.8 %branch_0_fun.1 = (f32[128,1024]{1,0:T(8,128)}, f32[128,1024]{1,0:T(8,128)}, f32[1,128]{1,0:T(1,128)}) custom-call(bf16[128,1024]{1,0:T(8,128)(2,1)S(1)} %get-tuple-element.33.img_local, bf16[128,1024]{1,0:T(8,128)(2,1)S(1)} %get-tuple-element.34.txt_local, bf16[1024,1024]{1,0:T(8,128)(2,1)S(1)} %get-tuple-element.35.img_head, ...), custom_call_target="tpu_custom_call" | custom-call | tf_op jit(solution)/shard_map/cond/branch_0_fun/pallas_call | solution.py:617
Async XLA Ops:
  1.9 48.3 %copy-start = (bf16[1024,1024]{1,0:T(8,128)(2,1)S(1)}, bf16[1024,1024]{1,0:T(8,128)(2,1)}, u32[]{:S(2)}) copy-start(bf16[1024,1024]{1,0:T(8,128)(2,1)} %img_head.1) | copy-start | bytes 6291460
  1.9 48.3 %copy-start.1 = (bf16[1024,1024]{1,0:T(8,128)(2,1)S(1)}, bf16[1024,1024]{1,0:T(8,128)(2,1)}, u32[]{:S(2)}) copy-start(bf16[1024,1024]{1,0:T(8,128)(2,1)} %txt_head.1) | copy-start | bytes 6291460
  1.9 48.3 %copy-start.2 = (bf16[128,1024]{1,0:T(8,128)(2,1)S(1)}, bf16[128,1024]{1,0:T(8,128)(2,1)}, u32[]{:S(2)}) copy-start(bf16[128,1024]{1,0:T(8,128)(2,1)} %img_feats.1) | copy-start | bytes 786436
  2.0 48.3 %copy-start.3 = (bf16[128,1024]{1,0:T(8,128)(2,1)S(1)}, bf16[128,1024]{1,0:T(8,128)(2,1)}, u32[]{:S(2)}) copy-start(bf16[128,1024]{1,0:T(8,128)(2,1)} %txt_feats.1) | copy-start | bytes 786436
  2.0 48.3 %copy-start.4 = (s32[128,1]{0,1:T(1,128)S(1)}, s32[128,1]{0,1:T(1,128)}, u32[]{:S(2)}) copy-start(s32[128,1]{0,1:T(1,128)} %param.14) | copy-start | bytes 1540
  2.0 48.3 %copy-start.5 = (s32[128]{0:T(128)S(1)}, s32[128]{0:T(128)}, u32[]{:S(2)}) copy-start(s32[128]{0:T(128)} %param.15) | copy-start | bytes 1540

commit v6 on v5

--- a/solution.py
+++ b/solution.py
@@ -602,9 +602,14 @@
     for kind, (local, head, out) in enumerate(
         ((img_local, img_head, out_img), (txt_local, txt_head, out_txt))
     ):
-        done[kind] = dot(local[...], head[...], 1, 1)
-        copies.append(pltpu.make_async_copy(done.at[kind], out, sems.at[kind]))
-        copies[-1].start()
+        half = head.shape[0] // 2
+        for n in range(2):
+            some = pl.ds(n * half, half)
+            done[kind, :, some] = dot(local[...], head[some], 1, 1)
+            copies.append(
+                pltpu.make_async_copy(done.at[kind, :, some], out.at[:, some], sems.at[kind, n])
+            )
+            copies[-1].start()
     out_loss[...] = loss[...]
     for copy in copies:
         copy.wait()
@@ -623,7 +628,7 @@
         ),
         in_specs=[vmem] * 5,
         out_specs=(away, away, vmem),
-        scratch_shapes=[pltpu.VMEM((2, pairs, deep), F32), pltpu.SemaphoreType.DMA((2,))],
+        scratch_shapes=[pltpu.VMEM((2, pairs, deep), F32), pltpu.SemaphoreType.DMA((2, 2))],
         compiler_params=pltpu.CompilerParams(vmem_limit_bytes=12 * 1024 * 1024),
     )(img_local, txt_local, img_head, txt_head, loss)
 

time: 53.7 us -> 53.6 us (level)
  no operation moved by 1% of the time
where the time goes in v6:
time: 53.6 us; the launch traced here: 53.4 us
  Pallas kernels  50.3 us (94%)
  between operations  2.83 us (5%)
    pallas_call x1, Pallas kernels, routed(): pl.pallas_call(functools.partial(kernel, slots), out_shape=(jax.ShapeDtyp...  47.6 us
    pallas_call x1, Pallas kernels, final(): pl.pallas_call(final_kernel, out_shape=(jax.ShapeDtypeStruct((pairs, deep...  2.76 us

profile of v6, /device:TPU:1, one launch (start us, length us, event | category | flops | bytes accessed | tf_op | source)
XLA Modules:
  0.0 53.4 jit_solution(1152769213845854177)
XLA Ops:
  1.9 0.0 copy-start
  1.9 0.0 copy-start.1
  1.9 0.0 copy-start.2
  2.0 0.0 copy-start.3
  2.0 0.0 copy-start.4
  2.0 0.0 copy-start.5
  2.0 47.6 %shard_map.105 = (bf16[128,1024]{1,0:T(8,128)(2,1)S(1)}, bf16[128,1024]{1,0:T(8,128)(2,1)S(1)}, f32[1,128]{1,0:T(1,128)S(1)}, s32[1]{0:T(128)}) custom-call(f32[1,1]{1,0:T(1,128)} %bitcast.7.scale_in, f32[1,1]{1,0:T(1,128)} %bitcast.8.bias_in, bf16[128,1024]{1,0:T(8,128)(2,1)} %img_feats.1, bf16[128,1024]{1,0:T(8,128)(2,1)} %txt_feats.1, ...), custom_call_target="tpu_custom_call" | custom-call | tf_op jit(solution)/shard_map/pallas_call | solution.py:544
  50.2 0.0 copy-done
  50.2 0.0 copy-done.1
  50.2 0.0 copy-done.2
  50.2 0.0 copy-done.3
  50.2 0.0 copy-done.4
  50.2 0.0 copy-done.5
  50.2 3.0 %conditional.1 = (f32[128,1024]{1,0:T(8,128)}, f32[128,1024]{1,0:T(8,128)}, f32[128]{0:T(128)}) conditional(s32[]{:T(128)} %bitcast.6, (bf16[128,1024]{1,0:T(8,128)(2,1)S(1)}, bf16[128,1024]{1,0:T(8,128)(2,1)S(1)}, bf16[1024,1024]{1,0:T(8,128)(2,1)S(1)}, bf16[1024,1024]{1,0:T(8,128)(2,1)S(1)}, f32[1,128]{1,0:T(1,128)S(1)}) %tuple.25, ...), branch_computations={%region_0.0_spmd, %region_1.0_spmd} | conditional | bytes 24 | solution.py:651
  50.3 2.8 %branch_0_fun.1 = (f32[128,1024]{1,0:T(8,128)}, f32[128,1024]{1,0:T(8,128)}, f32[1,128]{1,0:T(1,128)}) custom-call(bf16[128,1024]{1,0:T(8,128)(2,1)S(1)} %get-tuple-element.33.img_local, bf16[128,1024]{1,0:T(8,128)(2,1)S(1)} %get-tuple-element.34.txt_local, bf16[1024,1024]{1,0:T(8,128)(2,1)S(1)} %get-tuple-element.35.img_head, ...), custom_call_target="tpu_custom_call" | custom-call | tf_op jit(solution)/shard_map/cond/branch_0_fun/pallas_call | solution.py:622
Async XLA Ops:
  1.9 48.3 %copy-start = (bf16[1024,1024]{1,0:T(8,128)(2,1)S(1)}, bf16[1024,1024]{1,0:T(8,128)(2,1)}, u32[]{:S(2)}) copy-start(bf16[1024,1024]{1,0:T(8,128)(2,1)} %img_head.1) | copy-start | bytes 6291460
  1.9 48.3 %copy-start.1 = (bf16[1024,1024]{1,0:T(8,128)(2,1)S(1)}, bf16[1024,1024]{1,0:T(8,128)(2,1)}, u32[]{:S(2)}) copy-start(bf16[1024,1024]{1,0:T(8,128)(2,1)} %txt_head.1) | copy-start | bytes 6291460
  1.9 48.3 %copy-start.2 = (bf16[128,1024]{1,0:T(8,128)(2,1)S(1)}, bf16[128,1024]{1,0:T(8,128)(2,1)}, u32[]{:S(2)}) copy-start(bf16[128,1024]{1,0:T(8,128)(2,1)} %img_feats.1) | copy-start | bytes 786436
  2.0 48.3 %copy-start.3 = (bf16[128,1024]{1,0:T(8,128)(2,1)S(1)}, bf16[128,1024]{1,0:T(8,128)(2,1)}, u32[]{:S(2)}) copy-start(bf16[128,1024]{1,0:T(8,128)(2,1)} %txt_feats.1) | copy-start | bytes 786436
  2.0 48.3 %copy-start.4 = (s32[128,1]{0,1:T(1,128)S(1)}, s32[128,1]{0,1:T(1,128)}, u32[]{:S(2)}) copy-start(s32[128,1]{0,1:T(1,128)} %param.14) | copy-start | bytes 1540
  2.0 48.3 %copy-start.5 = (s32[128]{0:T(128)S(1)}, s32[128]{0:T(128)}, u32[]{:S(2)}) copy-start(s32[128]{0:T(128)} %param.15) | copy-start | bytes 1540
